TPU v7x, 32 devices: a whole 2x2x4 slice. The times are simulated.
32 devices in a mesh: dp: 4 (over z), seq: 4 (over y, x), mp: 2 (over core).
Axes of the slice: x: 2, y: 2, z: 4, core: 2. Of those that a mesh axis runs over, the one named last changes fastest.
Arguments:
- tokens: bfloat16 [2, 4, 2048, 768], P(None, 'dp', 'seq'), may hold values from -6 to 6
- output_cotangent: bfloat16 [2, 4, 2048, 768], P(None, 'dp', 'seq'), may hold values from -6 to 6
- document_numbers: int32 [2, 4, 2048], P(None, 'dp'), may hold values from 0 to 3, as said below
- document_adapter: int32 [2, 4, 4], P(None, 'dp'), may hold values from 0 to 7
- input_norm_gain: bfloat16 [2, 768], replicated, may hold values from 0.5 to 1.5
- gate_head_projection: bfloat16 [2, 768, 2, 1536], P(None, 'dp', None, 'mp'), may hold values from -0.21875 to 0.21875
- map_projection: bfloat16 [2, 768, 256], P(None, 'dp'), may hold values from -0.21875 to 0.21875
- step_projection: bfloat16 [2, 768, 24], P(None, 'dp', 'mp'), may hold values from -0.21875 to 0.21875
- output_projection: bfloat16 [2, 1536, 768], P(None, 'mp', 'dp'), may hold values from -0.15625 to 0.15625
- head_conv_taps: bfloat16 [2, 5, 1536], P(None, None, 'mp'), may hold values from -0.5 to 0.5
- map_conv_taps: bfloat16 [2, 5, 256], replicated, may hold values from -0.5 to 0.5
- head_settings: float32 [2, 3, 24], P(None, None, 'mp'), as said below
- gated_norm_gain: bfloat16 [2, 1536], P(None, 'mp'), may hold values from 0.5 to 1.5
- adapter_broad: float32 [2, 8, 16, 3, 1536], P(None, 'dp', None, None, 'mp'), may hold values from -0.3125 to 0.3125
- adapter_step: float32 [2, 8, 16, 24], P(None, 'dp', None, 'mp'), may hold values from -0.3125 to 0.3125
- adapter_shared: float32 [2, 8, 16, 1792], P(None, 'dp'), may hold values from -0.3125 to 0.3125
- broad_first_moment: float32 [2, 8, 16, 3, 1536], P(None, 'dp', None, None, 'mp'), may hold values from -0.0048828125 to 0.0048828125
- step_first_moment: float32 [2, 8, 16, 24], P(None, 'dp', None, 'mp'), may hold values from -0.0048828125 to 0.0048828125
- shared_first_moment: float32 [2, 8, 16, 1792], P(None, 'dp'), may hold values from -0.0048828125 to 0.0048828125
- broad_second_moment: float32 [2, 8, 16, 3, 1536], P(None, 'dp', None, None, 'mp'), may hold values from 6.080713e-07 to 2.432285e-06
- step_second_moment: float32 [2, 8, 16, 24], P(None, 'dp', None, 'mp'), may hold values from 6.080713e-07 to 2.432285e-06
- shared_second_moment: float32 [2, 8, 16, 1792], P(None, 'dp'), may hold values from 6.080713e-07 to 2.432285e-06
Outputs:
- mixed_out: bfloat16 [2, 4, 2048, 768], P(None, 'dp', 'seq')
- grad_tokens: bfloat16 [2, 4, 2048, 768], P(None, 'dp', 'seq')
- grad_norm: float32 [], replicated
- revised_broad: float32 [2, 8, 16, 3, 1536], P(None, 'dp', None, None, 'mp')
- revised_step: float32 [2, 8, 16, 24], P(None, 'dp', None, 'mp')
- revised_shared: float32 [2, 8, 16, 1792], P(None, 'dp')
- fresh_first_broad: float32 [2, 8, 16, 3, 1536], P(None, 'dp', None, None, 'mp')
- fresh_first_step: float32 [2, 8, 16, 24], P(None, 'dp', None, 'mp')
- fresh_first_shared: float32 [2, 8, 16, 1792], P(None, 'dp')
- fresh_square_broad: float32 [2, 8, 16, 3, 1536], P(None, 'dp', None, None, 'mp')
- fresh_square_step: float32 [2, 8, 16, 24], P(None, 'dp', None, 'mp')
- fresh_square_shared: float32 [2, 8, 16, 1792], P(None, 'dp')
- copy_wide: bfloat16 [2, 8, 16, 3, 1536], P(None, 'dp', None, None, 'mp')
- copy_dt: bfloat16 [2, 8, 16, 24], P(None, 'dp', None, 'mp')
- copy_rep: bfloat16 [2, 8, 16, 1792], P(None, 'dp')
Inputs may be any that keep to these rules, and one draw needn't show every extreme that they name: `document_numbers`: never falling along a pack and starting at 0. In each row one micro-batch, drawn from the seed, holds a single document; every other pack holds documents 0 to 3, the last of them at least half of the pack. `head_settings`: row 0 is the bias added before softplus, row 1 the logarithm of the decay coefficient, row 2 the skip factor.
All inputs are finite; a program needn't handle non-finite values.
Results may differ from a plain program's by a relative error of at most 0.025.
Values may be sent and summed in bfloat16 or wider, within the bound.
No kernel may reach another device: no remote copies, remote signals or barrier semaphores. Data moves between devices by JAX's collectives and lax.ppermute only.
A program may use at most 256 MiB of HBM per device.

v0:
```python
import jax
import jax.numpy as jnp
from jax import lax
from jax.sharding import PartitionSpec as P

CONV = 4
SPAN = 256
ADAPTER_COUNT = 8
STEP = 10


norm_eps = 1e-05
learn_rate = 0.04
beta_one = 0.5
beta_two = 0.5
weight_decay = 0.01
adam_eps = 1e-08
clip_max = 1.0
highest = lax.Precision.HIGHEST


def shifted(block, axis, distance):
    devices = range(lax.axis_size(axis))
    route = [(i - distance, i) for i in devices if i - distance in devices]
    return lax.ppermute(block, axis, route)


def carried_in(part, axis, combine, identity, reverse):
    count = lax.axis_size(axis)
    place = lax.axis_index(axis)
    ahead = count - 1 - place if reverse else place
    gathered = jax.tree.map(lambda a: lax.all_gather(a, axis), part)
    state = jax.tree.map(lambda a, e: jnp.zeros_like(a) + jnp.asarray(e, a.dtype), part, identity)

    def one(turn, state):
        source = count - 1 - turn if reverse else turn
        return combine(
            state, jax.tree.map(lambda a: lax.dynamic_index_in_dim(a, source, 0, False), gathered)
        )

    return lax.fori_loop(0, ahead, one, state)


def product(left_side, right_side):
    return jnp.dot(left_side, right_side, preferred_element_type=jnp.float32)


def product_back(left_side, right_side):
    return lax.dot_general(
        left_side, right_side, (((1,), (1,)), ((), ())), preferred_element_type=jnp.float32
    )


def product_left(left_side, right_side):
    return lax.dot_general(
        left_side, right_side, (((0,), (0,)), ((), ())), preferred_element_type=jnp.float32
    )


def pick_rank(values, adapter_pick):
    length = values.shape[0]
    return jnp.sum(
        values.reshape(length, adapter_pick.shape[1], -1) * adapter_pick[:, :, None], axis=1
    )


def spread_rank(values, adapter_pick):
    length = values.shape[0]
    spread = adapter_pick[:, :, None] * values.astype(jnp.float32)[:, None, :]
    return spread.reshape(length, -1).astype(jnp.bfloat16)


def join_states(earlier, later_part):
    return (earlier[0] * later_part[0], later_part[0][:, None, None] * earlier[1] + later_part[1])


def piece_ssd(x_heads, b_matrix, c_matrix, dt_value, decay_log, seg_own, prior_seg):
    length, head_count, head_width = x_heads.shape
    blocks = length // SPAN
    x_blocks = x_heads.reshape(blocks, SPAN, head_count, head_width)
    b_blocks = b_matrix.reshape(blocks, SPAN, -1)
    c_blocks = c_matrix.reshape(blocks, SPAN, -1)
    dt_blocks = dt_value.reshape(blocks, SPAN, head_count)
    seg_blocks = seg_own.reshape(blocks, SPAN)
    cumulated = jnp.cumsum(decay_log.reshape(blocks, SPAN, head_count), axis=1)
    positions = jnp.arange(SPAN)
    same_doc = (seg_blocks[:, :, None] == seg_blocks[:, None, :]) & (
        positions[:, None] >= positions[None, :]
    )[None]
    gaps_log = cumulated[:, :, None, :] - cumulated[:, None, :, :]
    mix_weight = jnp.where(
        same_doc[..., None], jnp.exp(jnp.where(same_doc[..., None], gaps_log, 0.0)), 0.0
    )
    scores = jnp.einsum("btn,bsn->bts", c_blocks, b_blocks, precision=highest)
    mixing = scores[..., None] * mix_weight * dt_blocks[:, None, :, :]
    intra_out = jnp.einsum("btsh,bshp->bthp", mixing, x_blocks, precision=highest)
    block_end = cumulated[:, SPAN - 1, :]
    end_seg = seg_blocks[:, SPAN - 1]
    tail_weight = (
        jnp.where(seg_blocks == end_seg[:, None], 1.0, 0.0)[..., None]
        * jnp.exp(block_end[:, None, :] - cumulated)
        * dt_blocks
    )
    block_state = jnp.einsum(
        "bshp,bsn->bhpn", tail_weight[..., None] * x_blocks, b_blocks, precision=highest
    )
    state_now = block_state[0]
    pieces_out = [intra_out[0]]
    entry = jnp.where(seg_blocks[1] == end_seg[0], 1.0, 0.0)[:, None] * jnp.exp(cumulated[1])
    from_before = jnp.einsum("tn,hpn->thp", c_blocks[1], state_now, precision=highest)
    pieces_out.append(intra_out[1] + entry[:, :, None] * from_before)
    keep_block = jnp.where(end_seg[1] == end_seg[0], 1.0, 0.0) * jnp.exp(block_end[1])
    state_now = keep_block[:, None, None] * state_now + block_state[1]
    offsets = jnp.cumsum(block_end, axis=0) - block_end
    total_cum = (cumulated + offsets[:, None, :]).reshape(length, head_count)
    carry_weight = jnp.where(seg_own == prior_seg, 1.0, 0.0)[:, None] * jnp.exp(total_cum)
    keep_total = jnp.where(seg_own[length - 1] == prior_seg, 1.0, 0.0) * jnp.exp(
        total_cum[length - 1]
    )
    return (jnp.concatenate(pieces_out, axis=0), state_now, keep_total, carry_weight)


def unpack_weights(big_weights, model_width):
    (
        gate_head_projection,
        map_projection,
        step_projection,
        output_projection,
        wide_part,
        dt_part,
        rep_part,
    ) = big_weights
    adapters, rank_width = (rep_part.shape[0], rep_part.shape[1])
    inner_local = output_projection.shape[0]
    state_width = map_projection.shape[1] // 2
    a_in = jnp.transpose(rep_part[:, :, :model_width], (2, 0, 1)).reshape(
        model_width, adapters * rank_width
    )
    b_zx = wide_part[:, :, 0:2].reshape(adapters * rank_width, 2 * inner_local)
    b_bc = rep_part[:, :, model_width : model_width + 2 * state_width].reshape(
        adapters * rank_width, 2 * state_width
    )
    b_dt = dt_part.reshape(adapters * rank_width, dt_part.shape[2])
    a_out = jnp.transpose(wide_part[:, :, 2], (2, 0, 1)).reshape(inner_local, adapters * rank_width)
    b_out = rep_part[:, :, model_width + 2 * state_width :].reshape(
        adapters * rank_width, model_width
    )
    w_zx_flat = gate_head_projection.reshape(model_width, 2 * inner_local)
    return (
        w_zx_flat,
        map_projection,
        step_projection,
        output_projection,
        a_in,
        b_zx,
        b_bc,
        b_dt,
        a_out,
        b_out,
    )


def layer_forward(residual, big_weights, small_weights, seg_ext, adapter_pick):
    length, model_width = residual.shape
    gain_vec, conv_taps, head_table, norm_vec = small_weights
    (
        w_zx_flat,
        map_projection,
        step_projection,
        output_projection,
        a_in,
        b_zx,
        b_bc,
        b_dt,
        a_out,
        b_out,
    ) = unpack_weights(big_weights, model_width)
    inner_local = output_projection.shape[0]
    heads_local = head_table.shape[1]
    head_width = inner_local // heads_local
    state_width = map_projection.shape[1] // 2
    scale_in = lax.rsqrt(jnp.mean(residual * residual, axis=-1, keepdims=True) + norm_eps)
    normed = (residual * scale_in * gain_vec[None, :]).astype(jnp.bfloat16)
    lowrank = pick_rank(product(normed, a_in), adapter_pick).astype(jnp.bfloat16)
    spread = spread_rank(lowrank, adapter_pick)
    zx_proj = product(normed, w_zx_flat) + product(spread, b_zx)
    bc_proj = product(normed, map_projection) + product(spread, b_bc)
    dt_raw = product(normed, step_projection) + product(spread, b_dt)
    gate_raw = zx_proj[:, :inner_local]
    mixer_rows = jnp.concatenate([zx_proj[:, inner_local:], bc_proj], axis=1).astype(jnp.bfloat16)
    before = shifted(mixer_rows[length - (CONV - 1) :], "seq", 1)
    extended = jnp.concatenate([before, mixer_rows], axis=0).astype(jnp.float32)
    seg_own = seg_ext[CONV - 1 :]
    prior_seg = seg_ext[CONV - 2]

    def local_mix(ext_rows, raw_steps):
        summed = conv_taps[CONV][None, :] + conv_taps[0][None, :] * ext_rows[CONV - 1 :]
        for offset in range(1, CONV):
            lower = CONV - 1 - offset
            same_doc = jnp.where(seg_ext[lower : lower + length] == seg_own, 1.0, 0.0)
            summed = (
                summed
                + conv_taps[offset][None, :] * ext_rows[lower : lower + length] * same_doc[:, None]
            )
        activated = jax.nn.silu(summed)
        x_heads = activated[:, :inner_local].reshape(length, heads_local, head_width)
        b_matrix = activated[:, inner_local : inner_local + state_width]
        c_matrix = activated[:, inner_local + state_width :]
        dt_value = jax.nn.softplus(raw_steps + head_table[0][None, :])
        decay_log = -jnp.exp(head_table[1])[None, :] * dt_value
        mixed, state_end, keep_total, carry_weight = piece_ssd(
            x_heads, b_matrix, c_matrix, dt_value, decay_log, seg_own, prior_seg
        )
        return (
            mixed + head_table[2][None, :, None] * x_heads,
            state_end,
            keep_total,
            carry_weight,
            c_matrix,
        )

    (mixed, state_end, keep_total, carry_weight, c_matrix), backward_map = jax.vjp(
        local_mix, extended, dt_raw
    )
    identity = (jnp.ones_like(keep_total), jnp.zeros_like(state_end))
    incoming = carried_in((keep_total, state_end), "seq", join_states, identity, False)[1]
    from_state = jnp.einsum("tn,hpn->thp", c_matrix, incoming, precision=highest)
    mixed = mixed + carry_weight[:, :, None] * from_state
    mixed_flat = mixed.reshape(length, inner_local)
    gate_act = jax.nn.silu(gate_raw)
    gated = mixed_flat * gate_act
    inner_all = inner_local * lax.axis_size("mp")
    squares = lax.psum(jnp.sum(gated * gated, axis=-1), "mp")
    scale_out = lax.rsqrt(squares / inner_all + norm_eps)
    normal_out = (gated * scale_out[:, None] * norm_vec[None, :]).astype(jnp.bfloat16)
    out_part = product(normal_out, output_projection)
    second_part = pick_rank(product(normal_out, a_out), adapter_pick)
    branch, second = lax.psum((out_part, second_part), "mp")
    spread_out = spread_rank(second.astype(jnp.bfloat16), adapter_pick)
    branch = branch + product(spread_out, b_out)
    saved = (
        residual,
        scale_in,
        normed,
        spread,
        gate_raw,
        backward_map,
        keep_total,
        carry_weight,
        c_matrix,
        incoming,
        from_state,
        mixed_flat,
        gate_act,
        gated,
        scale_out,
        normal_out,
        spread_out,
    )
    return (residual + branch, saved)


def layer_backward(upstream, saved, big_weights, small_weights, adapter_pick):
    (
        residual,
        scale_in,
        normed,
        spread,
        gate_raw,
        backward_map,
        keep_total,
        carry_weight,
        c_matrix,
        incoming,
        from_state,
        mixed_flat,
        gate_act,
        gated,
        scale_out,
        normal_out,
        spread_out,
    ) = saved
    length, model_width = residual.shape
    gain_vec, conv_taps, head_table, norm_vec = small_weights
    (
        w_zx_flat,
        map_projection,
        step_projection,
        output_projection,
        a_in,
        b_zx,
        b_bc,
        b_dt,
        a_out,
        b_out,
    ) = unpack_weights(big_weights, model_width)
    inner_local = output_projection.shape[0]
    heads_local = head_table.shape[1]
    head_width = inner_local // heads_local
    adapters = big_weights[6].shape[0]
    rank_width = big_weights[6].shape[1]
    inner_all = inner_local * lax.axis_size("mp")
    upstream_low = upstream.astype(jnp.bfloat16)
    grad_bout = product_left(spread_out, upstream_low)
    second_grad = pick_rank(product_back(upstream_low, b_out), adapter_pick).astype(jnp.bfloat16)
    second_spread = spread_rank(second_grad, adapter_pick)
    grad_normal = product_back(upstream_low, output_projection) + product_back(second_spread, a_out)
    grad_aout = product_left(normal_out, second_spread)
    weighted = grad_normal * norm_vec[None, :]
    inner_sum = lax.psum(jnp.sum(weighted * gated, axis=-1), "mp")
    grad_gated = (
        scale_out[:, None] * weighted - gated * (scale_out**3 * inner_sum / inner_all)[:, None]
    )
    sigmoid_gate = jax.nn.sigmoid(gate_raw)
    grad_gate = grad_gated * mixed_flat * sigmoid_gate * (1.0 + gate_raw * (1.0 - sigmoid_gate))
    grad_mixed = (grad_gated * gate_act).reshape(length, heads_local, head_width)
    weighted_grad = carry_weight[:, :, None] * grad_mixed
    own_state = jnp.einsum("thp,tn->hpn", weighted_grad, c_matrix, precision=highest)
    grad_weight = jnp.sum(grad_mixed * from_state, axis=-1)
    grad_cmat = jnp.einsum("thp,hpn->tn", weighted_grad, incoming, precision=highest)
    identity = (jnp.ones_like(keep_total), jnp.zeros_like(own_state))
    later_grad = carried_in((keep_total, own_state), "seq", join_states, identity, True)[1]
    grad_keep = jnp.sum(later_grad * incoming, axis=(1, 2))
    grad_ext, grad_raw = backward_map((grad_mixed, later_grad, grad_keep, grad_weight, grad_cmat))
    after = shifted(grad_ext[: CONV - 1], "seq", -1)
    padding = jnp.zeros((length - (CONV - 1), grad_ext.shape[1]), jnp.float32)
    grad_rows = grad_ext[CONV - 1 :] + jnp.concatenate([padding, after], axis=0)
    grad_zx = jnp.concatenate([grad_gate, grad_rows[:, :inner_local]], axis=1).astype(jnp.bfloat16)
    step_gradient = grad_raw.astype(jnp.bfloat16)
    lowrank_part = pick_rank(
        product_back(grad_zx, b_zx) + product_back(step_gradient, b_dt), adapter_pick
    )
    grad_bc, lowrank_part = lax.psum((grad_rows[:, inner_local:], lowrank_part), "mp")
    grad_bc = grad_bc.astype(jnp.bfloat16)
    lowrank_grad = (lowrank_part + pick_rank(product_back(grad_bc, b_bc), adapter_pick)).astype(
        jnp.bfloat16
    )
    lowrank_spread = spread_rank(lowrank_grad, adapter_pick)
    grad_bzx = product_left(spread, grad_zx)
    grad_bbc = product_left(spread, grad_bc)
    grad_bdt = product_left(spread, step_gradient)
    grad_ain = product_left(normed, lowrank_spread)
    shared_part = (product_back(grad_bc, map_projection) + product_back(lowrank_spread, a_in)) * (
        1.0 / lax.axis_size("mp")
    )
    grad_normed = (
        product_back(grad_zx, w_zx_flat)
        + product_back(step_gradient, step_projection)
        + shared_part
    )
    grad_normed = lax.psum(grad_normed, "mp")
    weighted_in = grad_normed * gain_vec[None, :]
    inner_in = jnp.sum(weighted_in * residual, axis=-1, keepdims=True)
    grad_resid = upstream + scale_in * weighted_in - residual * scale_in**3 * inner_in / model_width
    broad_gradient = jnp.concatenate(
        [
            grad_bzx.reshape(adapters, rank_width, 2, inner_local),
            jnp.transpose(grad_aout.reshape(inner_local, adapters, rank_width), (1, 2, 0))[
                :, :, None, :
            ],
        ],
        axis=2,
    )
    grad_dtpart = grad_bdt.reshape(adapters, rank_width, heads_local)
    shared_gradient = jnp.concatenate(
        [
            jnp.transpose(grad_ain.reshape(model_width, adapters, rank_width), (1, 2, 0)),
            grad_bbc.reshape(adapters, rank_width, -1),
            grad_bout.reshape(adapters, rank_width, model_width),
        ],
        axis=2,
    )
    return (grad_resid, (broad_gradient, grad_dtpart, shared_gradient))


def adamw_update(param_now, gradient, moment_now, square_now, scale_factor):
    gradient = gradient * scale_factor
    first_mom = beta_one * moment_now + (1.0 - beta_one) * gradient
    second_mom = beta_two * square_now + (1.0 - beta_two) * gradient * gradient
    update = (
        first_mom
        / (1.0 - beta_one**STEP)
        / (jnp.sqrt(second_mom / (1.0 - beta_two**STEP)) + adam_eps)
    )
    param_new = param_now - learn_rate * (update + weight_decay * param_now)
    return (param_new, first_mom, second_mom)


def per_device(
    tokens,
    output_cotangent,
    document_numbers,
    document_adapter,
    input_norm_gain,
    gate_head_projection,
    map_projection,
    step_projection,
    output_projection,
    head_conv_taps,
    map_conv_taps,
    head_settings,
    gated_norm_gain,
    adapter_broad,
    adapter_step,
    adapter_shared,
    broad_first_moment,
    step_first_moment,
    shared_first_moment,
    broad_second_moment,
    step_second_moment,
    shared_second_moment,
):
    batches = tokens.shape[0]
    length = tokens.shape[2]
    layers = gate_head_projection.shape[0]
    doc_count = document_adapter.shape[2]
    lowrank_broad = adapter_broad.astype(jnp.bfloat16)
    lowrank_step = adapter_step.astype(jnp.bfloat16)
    lowrank_shared = adapter_shared.astype(jnp.bfloat16)
    begin_position = lax.axis_index("seq") * length
    small_all = []
    for layer_index in range(layers):
        conv_taps = jnp.concatenate(
            [head_conv_taps[layer_index], map_conv_taps[layer_index]], axis=1
        ).astype(jnp.float32)
        small_all.append(
            (
                input_norm_gain[layer_index].astype(jnp.float32),
                conv_taps,
                head_settings[layer_index],
                gated_norm_gain[layer_index].astype(jnp.float32),
            )
        )
    totals = [None] * layers
    outputs = []
    input_grads = []
    for micro_index in range(batches):
        seg_pad = jnp.concatenate(
            [jnp.full((CONV - 1,), -1, jnp.int32), document_numbers[micro_index, 0]], axis=0
        )
        seg_ext = lax.dynamic_slice_in_dim(seg_pad, begin_position, length + CONV - 1)
        seg_own = seg_ext[CONV - 1 :]
        doc_pick = jnp.where(seg_own[:, None] == jnp.arange(doc_count)[None, :], 1.0, 0.0).astype(
            jnp.float32
        )
        which_pick = jnp.where(
            document_adapter[micro_index, 0][:, None] == jnp.arange(ADAPTER_COUNT)[None, :],
            1.0,
            0.0,
        ).astype(jnp.float32)
        adapter_pick = jnp.dot(doc_pick, which_pick, precision=highest)
        residual = tokens[micro_index, 0].astype(jnp.float32)
        kept = []
        for layer_index in range(layers):
            big_weights = (
                lax.all_gather(gate_head_projection[layer_index], "dp", axis=0, tiled=True),
                lax.all_gather(map_projection[layer_index], "dp", axis=0, tiled=True),
                lax.all_gather(step_projection[layer_index], "dp", axis=0, tiled=True),
                lax.all_gather(output_projection[layer_index], "dp", axis=1, tiled=True),
                lax.all_gather(lowrank_broad[layer_index], "dp", axis=0, tiled=True),
                lax.all_gather(lowrank_step[layer_index], "dp", axis=0, tiled=True),
                lax.all_gather(lowrank_shared[layer_index], "dp", axis=0, tiled=True),
            )
            residual, saved = layer_forward(
                residual, big_weights, small_all[layer_index], seg_ext, adapter_pick
            )
            kept.append((big_weights, saved))
        outputs.append(residual.astype(jnp.bfloat16))
        upstream = output_cotangent[micro_index, 0].astype(jnp.float32)
        for layer_index in reversed(range(layers)):
            big_weights, saved = kept[layer_index]
            upstream, layer_grads = layer_backward(
                upstream, saved, big_weights, small_all[layer_index], adapter_pick
            )
            if totals[layer_index] is None:
                totals[layer_index] = layer_grads
            else:
                totals[layer_index] = tuple(
                    (old + new for old, new in zip(totals[layer_index], layer_grads))
                )
        input_grads.append(upstream.astype(jnp.bfloat16))
    broad_gradient = jnp.stack([entry[0] for entry in totals], axis=0)
    step_gradient = jnp.stack([entry[1] for entry in totals], axis=0)
    shared_gradient = jnp.stack([entry[2] for entry in totals], axis=0)
    broad_gradient, step_gradient, shared_gradient = (
        lax.psum_scatter(broad_gradient, "dp", scatter_dimension=1, tiled=True),
        lax.psum_scatter(step_gradient, "dp", scatter_dimension=1, tiled=True),
        lax.psum_scatter(shared_gradient, "dp", scatter_dimension=1, tiled=True),
    )
    broad_gradient, step_gradient, shared_gradient = lax.psum(
        (broad_gradient, step_gradient, shared_gradient), "seq"
    )
    local_sq = (
        jnp.sum(broad_gradient * broad_gradient)
        + jnp.sum(step_gradient * step_gradient)
        + jnp.sum(shared_gradient * shared_gradient) / lax.axis_size("mp")
    )
    grad_norm = jnp.sqrt(lax.psum(local_sq, ("dp", "mp")))
    scale_factor = clip_max / jnp.maximum(grad_norm, clip_max)
    revised_broad, fresh_first_broad, fresh_square_broad = adamw_update(
        adapter_broad, broad_gradient, broad_first_moment, broad_second_moment, scale_factor
    )
    revised_step, fresh_first_step, fresh_square_step = adamw_update(
        adapter_step, step_gradient, step_first_moment, step_second_moment, scale_factor
    )
    revised_shared, fresh_first_shared, fresh_square_shared = adamw_update(
        adapter_shared, shared_gradient, shared_first_moment, shared_second_moment, scale_factor
    )
    mixed_out = jnp.stack(outputs, axis=0)[:, None]
    grad_tokens = jnp.stack(input_grads, axis=0)[:, None]
    return (
        mixed_out,
        grad_tokens,
        grad_norm,
        revised_broad,
        revised_step,
        revised_shared,
        fresh_first_broad,
        fresh_first_step,
        fresh_first_shared,
        fresh_square_broad,
        fresh_square_step,
        fresh_square_shared,
        revised_broad.astype(jnp.bfloat16),
        revised_step.astype(jnp.bfloat16),
        revised_shared.astype(jnp.bfloat16),
    )


def solution(mesh):
    placed = (
        P(None, "dp", "seq", None),
        P(None, "dp", "seq", None),
        P(None, "dp", None),
        P(None, "dp", None),
        P(),
        P(None, "dp", None, "mp"),
        P(None, "dp", None),
        P(None, "dp", "mp"),
        P(None, "mp", "dp"),
        P(None, None, "mp"),
        P(),
        P(None, None, "mp"),
        P(None, "mp"),
        P(None, "dp", None, None, "mp"),
        P(None, "dp", None, "mp"),
        P(None, "dp", None, None),
        P(None, "dp", None, None, "mp"),
        P(None, "dp", None, "mp"),
        P(None, "dp", None, None),
        P(None, "dp", None, None, "mp"),
        P(None, "dp", None, "mp"),
        P(None, "dp", None, None),
    )
    return jax.shard_map(
        per_device,
        mesh=mesh,
        in_specs=placed,
        out_specs=(
            P(None, "dp", "seq", None),
            P(None, "dp", "seq", None),
            P(),
            P(None, "dp", None, None, "mp"),
            P(None, "dp", None, "mp"),
            P(None, "dp", None, None),
            P(None, "dp", None, None, "mp"),
            P(None, "dp", None, "mp"),
            P(None, "dp", None, None),
            P(None, "dp", None, None, "mp"),
            P(None, "dp", None, "mp"),
            P(None, "dp", None, None),
            P(None, "dp", None, None, "mp"),
            P(None, "dp", None, "mp"),
            P(None, "dp", None, None),
        ),
        check_vma=False,
    )
```

profile of v0, /device:TPU:0, one launch (start us, length us, event | category | flops | bytes accessed | tf_op | source)
XLA Modules:
  0.0 1352.4 jit_solution(1823193877201676759)
XLA Ops:
  14.5 20.7 %all-gather.4 = bf16[1,768,12]{2,0,1:T(2,128)(2,1)S(1)} all-gather(bf16[1,192,12]{2,0,1:T(2,128)(2,1)S(1)} %copy.1338), channel_id=6, replica_groups=mesh['dp'=4,'seq'=4,'mp'=2] {'dp'}, dimensions={1}, use_global_device_ids=true | all-gather | bytes 23040 | tf_op jit(solution)/shard_map/all_gather | solution.py:458
  36.6 19.9 %all-gather.1 = bf16[1,8,16,1792]{3,2,0,1:T(8,128)(2,1)S(1)} all-gather(bf16[1,2,16,1792]{3,2,0,1:T(8,128)(2,1)S(1)} %get-tuple-element.901), channel_id=3, replica_groups=mesh['dp'=4,'seq'=4,'mp'=2] {'dp'}, dimensions={1}, use_global_device_ids=true | all-gather | bytes 573440 | tf_op jit(solution)/shard_map/all_gather | solution.py:462
  59.0 13.3 all-gather.5
  74.5 15.5 %all-gather.2 = bf16[1,8,16,3,768]{4,2,1,3,0:T(8,128)(2,1)S(1)} all-gather(bf16[1,2,16,3,768]{4,2,1,3,0:T(8,128)(2,1)S(1)} %get-tuple-element.899), channel_id=4, replica_groups=mesh['dp'=4,'seq'=4,'mp'=2] {'dp'}, dimensions={1}, use_global_device_ids=true | all-gather | bytes 737280 | tf_op jit(solution)/shard_map/all_gather | solution.py:460
  100.3 14.3 %all-gather.3 = bf16[1,768,256]{2,1,0:T(8,128)(2,1)S(1)} all-gather(bf16[1,192,256]{2,1,0:T(8,128)(2,1)S(1)} %get-tuple-element.903), channel_id=5, replica_groups=mesh['dp'=4,'seq'=4,'mp'=2] {'dp'}, dimensions={1}, use_global_device_ids=true | all-gather | bytes 491520 | tf_op jit(solution)/shard_map/all_gather | solution.py:457
  182.2 10.3 all-gather.20
  208.5 8.5 fusion.194
  265.6 19.4 %all-gather.11 = bf16[1,768,12]{2,0,1:T(2,128)(2,1)S(1)} all-gather(bf16[1,192,12]{2,0,1:T(2,128)(2,1)S(1)} %copy.1340), channel_id=13, replica_groups=mesh['dp'=4,'seq'=4,'mp'=2] {'dp'}, dimensions={1}, use_global_device_ids=true | all-gather | bytes 23040 | tf_op jit(solution)/shard_map/all_gather | solution.py:458
  285.9 19.9 %all-gather.9 = bf16[1,8,16,3,768]{4,2,1,3,0:T(8,128)(2,1)S(1)} all-gather(bf16[1,2,16,3,768]{4,2,1,3,0:T(8,128)(2,1)S(1)} %copy-done.232), channel_id=11, replica_groups=mesh['dp'=4,'seq'=4,'mp'=2] {'dp'}, dimensions={1}, use_global_device_ids=true | all-gather | bytes 737280 | tf_op jit(solution)/shard_map/all_gather | solution.py:460
  307.0 20.0 %all-gather.8 = bf16[1,8,16,1792]{3,2,0,1:T(8,128)(2,1)S(1)} all-gather(bf16[1,2,16,1792]{3,2,0,1:T(8,128)(2,1)S(1)} %copy-done.261), channel_id=10, replica_groups=mesh['dp'=4,'seq'=4,'mp'=2] {'dp'}, dimensions={1}, use_global_device_ids=true | all-gather | bytes 573440 | tf_op jit(solution)/shard_map/all_gather | solution.py:462
  329.9 14.0 %all-gather.12 = bf16[1,8,16,12]{3,2,0,1:T(8,128)(2,1)} all-gather(bf16[1,2,16,12]{3,2,0,1:T(8,128)(2,1)S(1)} %copy-done.444), channel_id=14, replica_groups=mesh['dp'=4,'seq'=4,'mp'=2] {'dp'}, dimensions={1}, use_global_device_ids=true | all-gather | bytes 3840 | tf_op jit(solution)/shard_map/all_gather | solution.py:461
  344.6 14.2 %all-gather.10 = bf16[1,768,256]{2,1,0:T(8,128)(2,1)S(1)} all-gather(bf16[1,192,256]{2,1,0:T(8,128)(2,1)S(1)} %copy-done.279), channel_id=12, replica_groups=mesh['dp'=4,'seq'=4,'mp'=2] {'dp'}, dimensions={1}, use_global_device_ids=true | all-gather | bytes 491520 | tf_op jit(solution)/shard_map/all_gather | solution.py:457
  422.9 10.8 all-gather.21
  505.1 18.8 %all-gather.37.cloned.1.call-done = f32[4,12,64,128]{3,2,1,0:T(8,128)} async-done(((f32[1,12,64,128]{3,2,1,0:T(8,128)}), f32[4,12,64,128]{3,2,1,0:T(8,128)}) %all-gather.37.cloned.1.call-update) | async-done | bytes 1572880 | tf_op jit(solution)/shard_map/all_gather | solution.py:32
  606.5 13.0 fusion.33
  619.6 11.1 fusion.37
  650.7 15.8 %all-gather.55.cloned.1.call-done = f32[48,64,128]{2,1,0:T(8,128)} async-done(((f32[12,64,128]{2,1,0:T(8,128)}), f32[48,64,128]{2,1,0:T(8,128)}) %all-gather.55.cloned.1.call-update) | async-done | bytes 1572880 | tf_op jit(solution)/shard_map/all_gather | solution.py:32
  880.1 13.3 fusion.35
  893.4 11.1 fusion.39
  926.0 10.9 all-gather.57.cloned.1.call-done
  1104.3 138.8 %all-reduce.94.cloned.1.call-done = (f32[2,8,16,3,768]{4,2,3,1,0:T(8,128)}, f32[2,8,16,1792]{3,2,1,0:T(8,128)}) async-done(((f32[2,8,16,3,768]{4,2,3,1,0:T(8,128)}, f32[2,8,16,1792]{3,2,1,0:T(8,128)}), (f32[2,8,16,3,768]{4,2,3,1,0:T(8,128)}, f32[2,8,16,1792]{3,2,1,0:T(8,128)})) %all-reduce.94.cloned.1.call-update) | async-done | bytes 4194320
  1255.5 18.1 %all-reduce.71 = f32[2,8,16,12]{2,0,3,1:T(2,128)S(1)} all-reduce(f32[2,8,16,12]{2,0,3,1:T(2,128)S(1)} %copy.1266), channel_id=21, replica_groups=mesh['dp'=4,'seq'=4,'mp'=2] {'dp'}, use_global_device_ids=true, to_apply=%region_151.153.clone | all-reduce | flops 3072 | bytes 24576
  1273.6 16.7 %psum.253 = f32[2,2,16,12]{2,0,3,1:T(2,128)S(1)} all-reduce(f32[2,2,16,12]{2,0,3,1:T(2,128)S(1)} %constant_dynamic-slice_fusion.1), channel_id=1, replica_groups=mesh['dp'=4,'seq'=4,'mp'=2] {'seq'}, use_global_device_ids=true, to_apply=%region_152.154 | all-reduce | flops 768 | bytes 6144 | tf_op jit(solution)/shard_map/psum | solution.py:490
  1304.4 16.9 %psum.255 = f32[]{:T(128)} all-reduce(f32[]{:T(128)S(6)} %add.1040), channel_id=1, replica_groups=mesh['dp'=4,'seq'=4,'mp'=2] {'dp','mp'}, use_global_device_ids=true, to_apply=%region_157.159 | all-reduce | flops 1 | bytes 8 | tf_op jit(solution)/shard_map/psum | solution.py:498
  (1773 shorter events, 861.3 us)
Async XLA Ops:
  7.2 115.2 %all-gather.43.cloned.1.call-start = ((), (), s32[]{:S(2)}) async-start(), calls=%async_computation.4 | async-start | bytes 2949120 | tf_op jit(solution)/shard_map/all_gather | solution.py:456
  10.5 222.9 %all-gather.39.cloned.1.call-start = ((), (), s32[]{:S(2)}) async-start(), calls=%async_computation.2 | async-start | bytes 1966080 | tf_op jit(solution)/shard_map/all_gather | solution.py:32
  129.3 7.8 collective-permute-start
  149.7 83.7 %all-gather.35.cloned.1.call-start = ((), (), s32[]{:S(2)}) async-start(), calls=%async_computation | async-start | bytes 1966080 | tf_op jit(solution)/shard_map/all_gather | solution.py:32
  169.7 89.6 %all-gather.45.cloned.1.call-start = ((), (), s32[]{:S(2)}) async-start(), calls=%async_computation.5 | async-start | bytes 1474560 | tf_op jit(solution)/shard_map/all_gather | solution.py:459
  171.6 187.2 %all-gather.49.cloned.1.call-start = ((), (), s32[]{:S(2)}) async-start(), calls=%async_computation.7 | async-start | bytes 1474560 | tf_op jit(solution)/shard_map/all_gather | solution.py:459
  172.2 192.0 %all-gather.47.cloned.1.call-start = ((), (), s32[]{:S(2)}) async-start(), calls=%async_computation.6 | async-start | bytes 2949120 | tf_op jit(solution)/shard_map/all_gather | solution.py:456
  172.8 203.5 %all-reduce.100.cloned.1.call-start = ((), (), s32[]{:S(2)}) async-start(), calls=%async_computation.16 | async-start | bytes 6291456 | tf_op jit(solution)/shard_map/psum | solution.py:238
  264.8 236.6 %all-gather.41.cloned.1.call-start = ((), (), s32[]{:S(2)}) async-start(), calls=%async_computation.3 | async-start | bytes 1966080 | tf_op jit(solution)/shard_map/all_gather | solution.py:32
  410.2 35.3 %collective-permute-start.1 = (bf16[3,1024]{1,0:T(4,128)(2,1)}, bf16[3,1024]{1,0:T(4,128)(2,1)}, u32[]{:S(2)}, u32[]{:S(2)}) collective-permute-start(bf16[3,1024]{1,0:T(4,128)(2,1)} %pad_maximum_fusion.17), channel_id=1, source_target_pairs={{0,2},{2,4},{4,6},{1,3},{3,5},{5,7},{8,10},{10,12},{12,14},{9,11},... | collective-permute-start | bytes 18440 | tf_op jit(solution)/shard_map/ppermute | solution.py:25
  417.4 29.4 %collective-permute-start.3 = (bf16[3,1024]{1,0:T(4,128)(2,1)S(1)}, bf16[3,1024]{1,0:T(4,128)(2,1)S(1)}, u32[]{:S(2)}, u32[]{:S(2)}) collective-permute-start(bf16[3,1024]{1,0:T(4,128)(2,1)S(1)} %pad_maximum_fusion.15), channel_id=1, source_target_pairs={{0,2},{2,4},{4,6},{1,3},{3,5},{5,7},{8,10},{10,12},{12,14},{9,11},... | collective-permute-start | bytes 18440 | tf_op jit(solution)/shard_map/ppermute | solution.py:25
  458.4 65.5 %all-gather.37.cloned.1.call-start = ((), (), s32[]{:S(2)}) async-start(), calls=%async_computation.1 | async-start | bytes 1966080 | tf_op jit(solution)/shard_map/all_gather | solution.py:32
  493.2 148.3 %all-gather.51.cloned.1.call-start = ((), (), s32[]{:S(2)}) async-start(), calls=%async_computation.8 | async-start | bytes 1966080 | tf_op jit(solution)/shard_map/all_gather | solution.py:32
  569.9 96.7 %all-gather.55.cloned.1.call-start = ((), (), s32[]{:S(2)}) async-start(), calls=%async_computation.10 | async-start | bytes 1966080 | tf_op jit(solution)/shard_map/all_gather | solution.py:32
  630.7 170.0 %all-reduce.98.cloned.1.call-start = ((), (), s32[]{:S(2)}) async-start(), calls=%async_computation.15 | async-start | bytes 6291456 | tf_op jit(solution)/shard_map/psum | solution.py:351
  741.9 5.6 collective-permute-start.6
  746.0 6.4 collective-permute-start.4
  775.9 140.3 %all-gather.53.cloned.1.call-start = ((), (), s32[]{:S(2)}) async-start(), calls=%async_computation.9 | async-start | bytes 1966080 | tf_op jit(solution)/shard_map/all_gather | solution.py:32
  841.0 95.9 %all-gather.57.cloned.1.call-start = ((), (), s32[]{:S(2)}) async-start(), calls=%async_computation.11 | async-start | bytes 1966080 | tf_op jit(solution)/shard_map/all_gather | solution.py:32
  904.6 338.5 %all-reduce.94.cloned.1.call-start = ((), (), s32[]{:S(2)}) async-start(), calls=%async_computation.13 | async-start | bytes 8388608
  1030.8 9.9 collective-permute-start.7
  1039.2 6.4 collective-permute-start.5
  1085.8 213.1 %all-reduce.92.cloned.1.call-start = ((), (), s32[]{:S(2)}) async-start(), calls=%async_computation.12 | async-start | bytes 2097152 | tf_op jit(solution)/shard_map/psum | solution.py:490
  1246.8 87.7 %all-reduce.96.cloned.1.call-start = ((), (), s32[]{:S(2)}) async-start(), calls=%async_computation.14 | async-start | bytes 12582912 | tf_op jit(solution)/shard_map/psum | solution.py:238
  (527 other events, 4354.1 us)
Sparse Core Ops, SparseCore 0:
  10.6 65.3 all-gather.42
  149.9 32.2 all-gather.38
  184.6 30.9 all-gather.34
  217.1 30.4 all-gather.44
  249.5 35.9 all-gather.48
  287.5 60.5 all-gather.46
  350.5 25.7 all-reduce.99
  458.5 30.4 all-gather.40
  493.3 30.4 all-gather.36
  570.0 35.7 all-gather.50
  630.9 35.6 all-gather.54
  776.0 24.7 all-reduce.97
  841.1 32.1 all-gather.52
  904.7 32.1 all-gather.56
  1085.9 157.0 all-reduce.93
  1247.0 51.8 all-reduce.91
  1302.3 32.2 all-reduce.95
where the time goes:
time: 1370 us; the launch traced here: 1350 us
  matrix products  365 us (27%)
  blocking collectives  285 us (21%)
  other arithmetic  234 us (17%)
  waiting for transfers between devices  212 us (15%)
  local copies, waits for them, and re-layouts  200 us (15%)
  between operations  30.2 us (2%)
  starting transfers between devices  25.4 us (2%)
    unnamed x18, waiting for transfers between devices  140 us
    dot_general x12, matrix products, piece_ssd(): jnp.einsum('btsh,bshp->bthp', mixing, x_blocks, precision=highest)  106 us
    unnamed x1094, local copies, waits for them, and re-layouts  58.4 us
    dot_general x40, matrix products, product_back(): lax.dot_general(left_side, right_side, (((1,), (1,)), ((), ())), preferre...  57.6 us
    another operation x32, other arithmetic  48.4 us
    dot_general x40, matrix products, product(): return jnp.dot(left_side, right_side, preferred_element_type=jnp.float32)  46.5 us
    all_gather x8, waiting for transfers between devices, carried_in(): gathered = jax.tree.map(lambda a: lax.all_gather(a, axis), part)  45.5 us
    all_gather x2, blocking collectives, per_device(): lax.all_gather(step_projection[layer_index], 'dp', axis=0, tiled=True)  40.1 us
  transfers between devices with their start and end apart: 25, of which 12 were waited for; matrix products, arithmetic and copies ran while one was open for 30% of the time, Pallas kernels for 0%

commit v1 on v0

v1 whole, which is shorter than its diff:
```python
import functools

import jax
import jax.numpy as jnp
from jax import lax
from jax.experimental import pallas as pl
from jax.experimental.pallas import tpu as pltpu
from jax.sharding import PartitionSpec as P

CONV = 4
STEP = 10
LANES = 128
SPAN = 128
PAD = 8
RESET = -128.0

norm_eps = 1e-05
learn_rate = 0.04
beta_one = 0.5
beta_two = 0.5
weight_decay = 0.01
adam_eps = 1e-08
clip_max = 1.0
low = jnp.bfloat16
full = jnp.float32


def nn(a, b):
    return lax.dot_general(a, b, (((1,), (0,)), ((), ())), preferred_element_type=full)


def nt(a, b):
    return lax.dot_general(a, b, (((1,), (1,)), ((), ())), preferred_element_type=full)


def tn(a, b):
    return lax.dot_general(a, b, (((0,), (0,)), ((), ())), preferred_element_type=full)


def two_parts(values, axis):
    high = values.astype(low)
    rest = (values - high.astype(full)).astype(low)
    return jnp.concatenate([high, rest], axis=axis)


def three_parts(values, axis):
    high = values.astype(low)
    rest = values - high.astype(full)
    middle = rest.astype(low)
    last = (rest - middle.astype(full)).astype(low)
    return jnp.concatenate([high, middle, last], axis=axis)


def widen(values, spread_two):
    return nn(two_parts(values, 1), spread_two)


def per_head(values, spread_two):
    heads = spread_two[:LANES]
    high = values.astype(low)
    rest = (values - high.astype(full)).astype(low)
    return nt(high, heads) + nt(rest, heads)


def triangle(kind):
    rows = lax.broadcasted_iota(jnp.int32, (SPAN, SPAN), 0)
    columns = lax.broadcasted_iota(jnp.int32, (SPAN, SPAN), 1)
    return rows >= columns if kind == "lower" else rows <= columns


def cumulate(values, kind):
    keep = triangle(kind).astype(full).astype(low)
    return nn(jnp.concatenate([keep, keep, keep], axis=1), three_parts(values, 0))


def sigmoid(values):
    return 1.0 / (1.0 + jnp.exp(-values))


def kernel_call(body, outs, ins, scratch=(), flops=0, name=None, limit=48):
    moved = sum(a.size * a.dtype.itemsize for a in list(ins) + list(outs))
    whole = pl.BlockSpec(memory_space=pltpu.VMEM)
    return pl.pallas_call(
        body,
        out_shape=tuple(outs),
        in_specs=[whole] * len(ins),
        out_specs=tuple([whole] * len(outs)),
        scratch_shapes=list(scratch),
        compiler_params=pltpu.CompilerParams(vmem_limit_bytes=limit * 2**20),
        cost_estimate=pl.CostEstimate(flops=flops, bytes_accessed=moved, transcendentals=0),
        name=name,
    )(*ins)


def shape(dims, kind):
    return jax.ShapeDtypeStruct(dims, kind)


def project_kernel(halves, half, h, gain, mask, w_in, adapt, normed_o, spread_o, gate_o, rows_o, dt_o):
    values = h[...].astype(full)
    width = values.shape[1]
    scale = lax.rsqrt(jnp.mean(values * values, axis=1, keepdims=True) + norm_eps)
    normed = (values * scale * gain[0:1]).astype(low)
    normed_o[...] = normed
    first = 3 * half + 2 * LANES
    part = width // halves
    down = jnp.concatenate([adapt[m, :, first : first + part] for m in range(halves)], axis=1)
    spread = nt(normed, down).astype(low) * mask[...]
    spread_o[...] = spread
    inner = halves * half
    for m in range(halves):
        for begin, end, target, place in (
            (0, half, gate_o, m * half),
            (half, 2 * half, rows_o, m * half),
            (2 * half, 2 * half + LANES, rows_o, inner + m * LANES),
        ):
            made = nn(normed, w_in[m, :, begin:end]) + nn(spread, adapt[m, :, begin:end])
            target[:, place : place + end - begin] = made.astype(target.dtype)
    begin = 2 * half + LANES
    w_dt = sum(w_in[m, :, begin : begin + LANES].astype(full) for m in range(halves)).astype(low)
    b_dt = sum(adapt[m, :, begin : begin + LANES].astype(full) for m in range(halves)).astype(low)
    dt_o[...] = nn(normed, w_dt) + nn(spread, b_dt)


def conv_chunk(ext, lags, taps, begin, columns):
    window = ext[pl.ds(begin, SPAN + PAD), columns]
    summed = taps[CONV : CONV + 1, columns] + taps[0:1, columns] * window[PAD:]
    for lag in range(1, CONV):
        same = lags[pl.ds(begin, SPAN), (lag - 1) * LANES : lag * LANES]
        summed = summed + taps[lag : lag + 1, columns] * window[PAD - lag : PAD - lag + SPAN] * same
    return summed


def fill_extended(ext, halo, rows):
    ext[0:PAD, :] = halo[...].astype(full)
    ext[PAD : PAD + rows.shape[0], :] = rows[...].astype(full)


def states_kernel(
    inner, rows, halo, taps, lags, dt_raw, table, jump, spread_two,
    act_o, xdt_o, dt_o, cum_o, flat_o, begin_o, end_o, total_o, ext, state,
):
    length = rows.shape[0]
    channels = rows.shape[1]
    fill_extended(ext, halo, rows)
    state[...] = jnp.zeros_like(state)

    def block(k, so_far):
        begin = pl.multiple_of(k * SPAN, SPAN)
        span = pl.ds(begin, SPAN)
        for c in range(0, channels, LANES):
            columns = slice(c, c + LANES)
            summed = conv_chunk(ext, lags, taps, begin, columns)
            act_o[span, columns] = (summed * sigmoid(summed)).astype(low)
        raw = dt_raw[span, :] + table[0:1, :]
        dt = jnp.maximum(raw, 0.0) + jnp.log1p(jnp.exp(-jnp.abs(raw)))
        cum = cumulate(jump[span, :] - jnp.exp(table[1:2, :]) * dt, "lower")
        dt_o[span, :] = dt
        cum_o[span, :] = cum
        flat_o[:, span] = cum.T
        total = cum[SPAN - 1 : SPAN, :]
        xdt = (act_o[span, 0:inner].astype(full) * widen(dt, spread_two[...])).astype(low)
        xdt_o[span, :] = xdt
        tail = widen(jnp.exp(total - cum), spread_two[...])
        b_map = act_o[span, inner : inner + LANES]
        begin_o[k] = state[...].astype(low)
        keep = widen(jnp.broadcast_to(jnp.exp(total), (8, LANES)), spread_two[...])[0:1]
        state[...] = state[...] * keep + tn(b_map, (xdt.astype(full) * tail).astype(low))
        return so_far + total

    total = lax.fori_loop(0, length // SPAN, block, jnp.zeros((1, LANES), full))
    end_o[...] = state[...].astype(low)
    total_o[...] = jnp.broadcast_to(total, total_o.shape)


def intra_kernel(inner, head_width, act, xdt, cum, flat, begin_state, skip, spread_two, y_o):
    length = act.shape[0]
    keep = triangle("lower")
    left = lax.broadcasted_iota(jnp.int32, (SPAN, LANES), 1) < head_width

    def block(k, carry):
        begin = pl.multiple_of(k * SPAN, SPAN)
        span = pl.ds(begin, SPAN)
        b_map = act[span, inner : inner + LANES]
        c_map = act[span, inner + LANES : inner + 2 * LANES]
        scores = nt(c_map, b_map)
        cum_now = cum[span, :]
        entry = widen(jnp.exp(cum_now), spread_two[...])
        before = nn(c_map, begin_state[k])
        for pair in range(inner // LANES):
            columns = slice(pair * LANES, (pair + 1) * LANES)
            mixing = []
            for head in (2 * pair, 2 * pair + 1):
                gap = cum_now[:, head : head + 1] - flat[head : head + 1, span]
                mixing.append((scores * jnp.exp(jnp.where(keep, gap, -1e30))).astype(low))
            x_pair = xdt[span, columns]
            nothing = jnp.zeros_like(x_pair)
            x_two = jnp.concatenate([jnp.where(left, x_pair, nothing), jnp.where(left, nothing, x_pair)], axis=0)
            intra = nn(jnp.concatenate(mixing, axis=1), x_two)
            y_o[span, columns] = (
                intra
                + entry[:, columns] * before[:, columns]
                + skip[0:1, columns] * act[span, columns].astype(full)
            ).astype(low)
        return carry

    lax.fori_loop(0, length // SPAN, block, 0)


def combine(parts, weights_log, spread_two):
    weights = widen(jnp.exp(weights_log), spread_two)
    total = parts[0].astype(full) * weights[0:1]
    for i in range(1, len(parts)):
        total = total + parts[i].astype(full) * weights[i : i + 1]
    return total


def output_kernel(
    halves, half, count, last, h, y_local, gate, act, cum, carry_log, gain, mask, w_out, adapt, spread_two, *rest
):
    parts, rest = rest[:count], rest[count:]
    h_o, y_o, normal_o, spread_o, coming_o, gated_s = rest
    length = h.shape[0]
    inner = halves * half
    coming = combine([p[...] for p in parts], carry_log[...], spread_two[...]).astype(low)
    coming_o[...] = coming
    before = jnp.zeros((1, LANES), full)
    for k in range(length // SPAN):
        span = slice(k * SPAN, (k + 1) * SPAN)
        cum_now = cum[span, :]
        carry = widen(jnp.exp(cum_now + before), spread_two[...])
        before = before + cum_now[SPAN - 1 : SPAN, :]
        c_map = act[span, inner + LANES : inner + 2 * LANES]
        y = y_local[span, :].astype(full) + carry * nn(c_map, coming)
        y_o[span, :] = y.astype(low)
        z = gate[span, :].astype(full)
        gated = y * z * sigmoid(z)
        scale = lax.rsqrt(jnp.mean(gated * gated, axis=1, keepdims=True) + norm_eps)
        normal_o[span, :] = (gated * scale * gain[0:1]).astype(low)
    place = 2 * half + 2 * LANES
    second = jnp.zeros((length, LANES), full)
    for m in range(halves):
        second = second + nt(normal_o[:, m * half : (m + 1) * half], adapt[m, :, place : place + half])
    spread = second.astype(low) * mask[...]
    spread_o[...] = spread
    width = h.shape[1]
    part = width // halves
    first = 3 * half + 2 * LANES + part
    up = jnp.concatenate([adapt[m, :, first : first + part] for m in range(halves)], axis=1)
    branch = nn(spread, up)
    for m in range(halves):
        branch = branch + nt(normal_o[:, m * half : (m + 1) * half], w_out[m])
    h_o[...] = (h[...].astype(full) + branch).astype(h_o.dtype)


def output_back_kernel(
    halves, half, upstream, y, gate, normal, spread_out, act, cum, gain, mask, w_out, adapt, spread_two,
    dgate_o, dy_o, own_o, down_o, up_o, seconds,
):
    length = y.shape[0]
    inner = halves * half
    width = upstream.shape[1]
    part = width // halves
    up_low = upstream[...].astype(low)
    place = 2 * half + 2 * LANES
    first = 3 * half + 2 * LANES + part
    up = jnp.concatenate([adapt[m, :, first : first + part] for m in range(halves)], axis=1)
    second = nt(up_low, up).astype(low) * mask[...]
    seconds[...] = second
    up_grad = tn(spread_out[...], up_low)
    for m in range(halves):
        up_o[m] = up_grad[:, m * part : (m + 1) * part].astype(up_o.dtype)
        down_o[m] = tn(second, normal[:, m * half : (m + 1) * half]).astype(down_o.dtype)
    own = jnp.zeros((LANES, inner), full)
    before = jnp.zeros((1, LANES), full)
    for k in range(length // SPAN):
        span = slice(k * SPAN, (k + 1) * SPAN)
        up_now = up_low[span]
        grads = []
        for m in range(halves):
            grads.append(nn(up_now, w_out[m]) + nn(seconds[span, :], adapt[m, :, place : place + half]))
        weighted = jnp.concatenate(grads, axis=1) * gain[0:1]
        y_now = y[span, :].astype(full)
        z = gate[span, :].astype(full)
        sig = sigmoid(z)
        silu = z * sig
        gated = y_now * silu
        scale = lax.rsqrt(jnp.mean(gated * gated, axis=1, keepdims=True) + norm_eps)
        mean_in = jnp.mean(weighted * gated, axis=1, keepdims=True)
        grad_gated = scale * weighted - gated * (scale * scale * scale * mean_in)
        dgate_o[span, :] = (grad_gated * y_now * sig * (1.0 + z * (1.0 - sig))).astype(low)
        dy = grad_gated * silu
        dy_o[span, :] = dy.astype(low)
        cum_now = cum[span, :]
        carry = widen(jnp.exp(cum_now + before), spread_two[...])
        before = before + cum_now[SPAN - 1 : SPAN, :]
        own = own + tn(act[span, inner + LANES : inner + 2 * LANES], (carry * dy).astype(low))
    own_o[...] = own.astype(low)


def intra_back_kernel(inner, head_width, act, xdt, dy, cum, flat, u_o, db_o, dc_o):
    length = act.shape[0]
    keep = triangle("upper")
    left = lax.broadcasted_iota(jnp.int32, (SPAN, LANES), 1) < head_width

    def block(k, carry):
        begin = pl.multiple_of(k * SPAN, SPAN)
        span = pl.ds(begin, SPAN)
        b_map = act[span, inner : inner + LANES]
        c_map = act[span, inner + LANES : inner + 2 * LANES]
        scores = nt(b_map, c_map)
        cum_now = cum[span, :]
        dscores = jnp.zeros((SPAN, SPAN), full)
        for pair in range(inner // LANES):
            columns = slice(pair * LANES, (pair + 1) * LANES)
            dy_pair = dy[span, columns]
            nothing = jnp.zeros_like(dy_pair)
            dy_two = jnp.concatenate([jnp.where(left, dy_pair, nothing), jnp.where(left, nothing, dy_pair)], axis=0)
            products = nt(xdt[span, columns], dy_two)
            mixing = []
            for i, head in enumerate((2 * pair, 2 * pair + 1)):
                gap = flat[head : head + 1, span] - cum_now[:, head : head + 1]
                decay = jnp.exp(jnp.where(keep, gap, -1e30))
                mixing.append((scores * decay).astype(low))
                dscores = dscores + products[:, i * SPAN : (i + 1) * SPAN] * decay
            u_o[span, columns] = nn(jnp.concatenate(mixing, axis=1), dy_two).astype(low)
        dlow = dscores.astype(low)
        db_o[span, :] = nn(dlow, c_map)
        dc_o[span, :] = tn(dlow, b_map)
        return carry

    lax.fori_loop(0, length // SPAN, block, 0)


def scan_back_kernel(
    inner, count, rows, halo, taps, lags, act, xdt, dy, y, u, db_in, dc_in, dt, cum, dt_raw, table, skip,
    begin_state, coming, carry_log, spread_two, *rest,
):
    parts, rest = rest[:count], rest[count:]
    dconv_o, ddt_o, ext, grad, dact = rest
    length = act.shape[0]
    channels = rows.shape[1]
    blocks = length // SPAN
    fill_extended(ext, halo, rows)
    grad[...] = combine([p[...] for p in parts], carry_log[...], spread_two[...])
    ends = [cum[(k + 1) * SPAN - 1 : (k + 1) * SPAN, :] for k in range(blocks)]
    for k in reversed(range(blocks)):
        span = slice(k * SPAN, (k + 1) * SPAN)
        cum_now = cum[span, :]
        total = ends[k]
        before = sum(ends[:k], jnp.zeros((1, LANES), full))
        b_map = act[span, inner : inner + LANES]
        c_map = act[span, inner + LANES : inner + 2 * LANES]
        grad_low = grad[...].astype(low)
        tail = widen(jnp.exp(total - cum_now), spread_two[...])
        entry = widen(jnp.exp(cum_now), spread_two[...])
        rows_wide = widen(jnp.exp(jnp.concatenate([total, before] * 4, axis=0)), spread_two[...])
        keep, carry = rows_wide[0:1], rows_wide[1:2]
        x = act[span, 0:inner].astype(full)
        x_dt = xdt[span, :].astype(full)
        from_later = tail * nn(b_map, grad_low)
        v = u[span, :].astype(full) + from_later
        state = begin_state[k].astype(full) + carry * coming[...].astype(full)
        dy_now = dy[span, :].astype(full)
        db = db_in[span, :] + nt((x_dt * tail).astype(low), grad_low)
        entry_dy = (entry * dy_now).astype(low)
        dc = dc_in[span, :] + nt(entry_dy, state.astype(low))
        kept = keep * grad[...]
        end_rows = jnp.sum(x_dt * from_later, axis=0, keepdims=True) + jnp.sum(kept * state, axis=0, keepdims=True)
        grad[...] = kept + tn(c_map, entry_dy)
        y_scan = y[span, :].astype(full) - skip[0:1, :] * x
        dcum = per_head(dy_now * y_scan - x_dt * v, spread_two[...])
        at_end = per_head(jnp.broadcast_to(end_rows, (8, inner)), spread_two[...])[0:1]
        ddecay = cumulate(dcum, "upper") + at_end
        raw = dt_raw[span, :] + table[0:1, :]
        ddt = per_head(x * v, spread_two[...]) - ddecay * jnp.exp(table[1:2, :])
        ddt_o[span, :] = (ddt * sigmoid(raw)).astype(low)
        dact[span, 0:inner] = widen(dt[span, :], spread_two[...]) * v + skip[0:1, :] * dy_now
        dact[span, inner : inner + LANES] = db
        dact[span, inner + LANES : inner + 2 * LANES] = dc
        for c in range(0, channels, LANES):
            columns = slice(c, c + LANES)
            summed = conv_chunk(ext, lags, taps, k * SPAN, columns)
            sig = sigmoid(summed)
            dconv_o[span, columns] = (dact[span, columns] * sig * (1.0 + summed * (1.0 - sig))).astype(low)


def gate_back_kernel(halves, half, dgate, spread, w_in, adapt, dn_o, dl_o, grad_o):
    dn = dl = 0.0
    for m in range(halves):
        piece = dgate[:, m * half : (m + 1) * half]
        dn = dn + nt(piece, w_in[m, :, 0:half])
        dl = dl + nt(piece, adapt[m, :, 0:half])
        grad_o[m] = tn(spread[...], piece).astype(grad_o.dtype)
    dn_o[...] = dn
    dl_o[...] = dl


def project_back_kernel(
    halves, half, upstream, h, gain, mask, dconv, after, taps, lags, ddt, dn_in, dl_in, spread, normed, w_in, adapt,
    dh_o, grad_o, down_o, ext, drows,
):
    length = h.shape[0]
    channels = dconv.shape[1]
    inner = halves * half
    ext[0:length, :] = dconv[...].astype(full)
    ext[length : length + PAD, :] = after[...].astype(full)

    def block(k, carry):
        begin = pl.multiple_of(k * SPAN, SPAN)
        span = pl.ds(begin, SPAN)
        for c in range(0, channels, LANES):
            columns = slice(c, c + LANES)
            window = ext[pl.ds(begin, SPAN + PAD), columns]
            total = taps[0:1, columns] * window[:SPAN]
            for lag in range(1, CONV):
                same = lags[span, (lag - 1) * LANES : lag * LANES]
                total = total + taps[lag : lag + 1, columns] * window[lag : lag + SPAN] * same
            drows[span, columns] = total.astype(low)
        return carry

    lax.fori_loop(0, length // SPAN, block, 0)
    dn, dl = dn_in[...], dl_in[...]
    begin = 2 * half + LANES
    step = ddt[...]
    w_dt = sum(w_in[m, :, begin : begin + LANES].astype(full) for m in range(halves)).astype(low)
    b_dt = sum(adapt[m, :, begin : begin + LANES].astype(full) for m in range(halves)).astype(low)
    dn = dn + nt(step, w_dt)
    dl = dl + nt(step, b_dt)
    step_grad = tn(spread[...], step).astype(grad_o.dtype)
    for m in range(halves):
        for first, last, place in (
            (half, 2 * half, m * half),
            (2 * half, 2 * half + LANES, inner + m * LANES),
        ):
            piece = drows[:, place : place + last - first]
            dn = dn + nt(piece, w_in[m, :, first:last])
            dl = dl + nt(piece, adapt[m, :, first:last])
            grad_o[m, :, first - half : last - half] = tn(spread[...], piece).astype(grad_o.dtype)
        grad_o[m, :, half + LANES : half + 2 * LANES] = step_grad
    back = dl.astype(low) * mask[...]
    width = h.shape[1]
    part = width // halves
    place = 3 * half + 2 * LANES
    for m in range(halves):
        down_o[m] = tn(back, normed[:, m * part : (m + 1) * part]).astype(down_o.dtype)
    down = jnp.concatenate([adapt[m, :, place : place + part] for m in range(halves)], axis=1)
    dn = dn + nn(back, down)
    values = h[...].astype(full)
    scale = lax.rsqrt(jnp.mean(values * values, axis=1, keepdims=True) + norm_eps)
    weighted = dn * gain[0:1]
    mean_in = jnp.mean(weighted * values, axis=1, keepdims=True)
    dh = upstream[...].astype(full) + scale * weighted - values * (scale * scale * scale * mean_in)
    dh_o[...] = dh.astype(dh_o.dtype)


def moved(block, axis, distance, wrap=False):
    count = lax.axis_size(axis)
    route = [(i, (i + distance) % count) for i in range(count) if wrap or 0 <= i + distance < count]
    return lax.ppermute(block, axis, route)


def swapped(block):
    count = lax.axis_size("mp")
    return lax.ppermute(block, "mp", [(i, count - 1 - i) for i in range(count)])


def summed_shares(parts, axis):
    count = lax.axis_size(axis)
    place = lax.axis_index(axis)
    total = lax.dynamic_index_in_dim(parts, place, 0, False).astype(full)
    for distance in range(1, count):
        piece = lax.dynamic_index_in_dim(parts, (place + distance) % count, 0, False)
        total = total + moved(piece, axis, distance, True).astype(full)
    return total


def reduced(gradient):
    mine = lax.axis_index("mp")
    keep = lax.dynamic_index_in_dim(gradient, mine, 0, False)
    give = lax.dynamic_index_in_dim(gradient, 1 - mine, 0, False)
    both = (keep.astype(full) + swapped(give).astype(full)).astype(low)
    owners, pieces = lax.axis_size("dp"), lax.axis_size("seq")
    ranks, columns = both.shape
    shares = both.reshape(owners, pieces, ranks // (owners * pieces), columns)
    over_seq = summed_shares(jnp.moveaxis(shares, 1, 0), "seq").astype(low)
    return summed_shares(over_seq, "dp")


def adamw_update(param_now, gradient, moment_now, square_now, scale_factor):
    gradient = gradient * scale_factor
    first_mom = beta_one * moment_now + (1.0 - beta_one) * gradient
    second_mom = beta_two * square_now + (1.0 - beta_two) * gradient * gradient
    update = (
        first_mom
        / (1.0 - beta_one**STEP)
        / (jnp.sqrt(second_mom / (1.0 - beta_two**STEP)) + adam_eps)
    )
    param_new = param_now - learn_rate * (update + weight_decay * param_now)
    return (param_new, first_mom, second_mom)


def lanes_of(values, place):
    room = jnp.zeros(values.shape[:-1] + (LANES,), values.dtype)
    return lax.dynamic_update_slice_in_dim(room, values, place, values.ndim - 1)


def rows_of(values, count=PAD):
    return jnp.concatenate([values, jnp.zeros((count - values.shape[0],) + values.shape[1:], values.dtype)], axis=0)


def per_device(
    tokens,
    output_cotangent,
    document_numbers,
    document_adapter,
    input_norm_gain,
    gate_head_projection,
    map_projection,
    step_projection,
    output_projection,
    head_conv_taps,
    map_conv_taps,
    head_settings,
    gated_norm_gain,
    adapter_broad,
    adapter_step,
    adapter_shared,
    broad_first_moment,
    step_first_moment,
    shared_first_moment,
    broad_second_moment,
    step_second_moment,
    shared_second_moment,
):
    halves = lax.axis_size("mp")
    pieces = lax.axis_size("seq")
    owners = lax.axis_size("dp")
    core = lax.axis_index("mp")
    place = lax.axis_index("seq")
    length, width = tokens.shape[2:]
    layers, _, _, half = gate_head_projection.shape
    inner = halves * half
    heads_local = head_settings.shape[2]
    heads = halves * heads_local
    head_width = inner // heads
    own_adapters, rank = adapter_broad.shape[1:3]
    own_rows = own_adapters * rank
    adapters = own_adapters * owners
    ranks = adapters * rank
    part = width // halves
    states = map_projection.shape[2] // 2
    channels = inner + 2 * states

    def mine(values):
        return lax.dynamic_index_in_dim(values, core, 0, False)

    h_first = mine(tokens)[0]
    cotangent = mine(output_cotangent)[0]
    documents = mine(document_numbers)[0]
    chosen = mine(document_adapter)[0]

    def gathered(block):
        got = lax.all_gather(block, ("mp", "dp"), axis=0, tiled=True)
        return got.reshape(halves, -1, block.shape[1])

    low_broad = adapter_broad.astype(low)
    low_step = adapter_step.astype(low)
    low_shared = adapter_shared.astype(low)
    weights = []
    for layer in range(layers):
        zx = gate_head_projection[layer]
        maps = lax.dynamic_slice_in_dim(map_projection[layer], core * states, states, 1)
        steps = lanes_of(step_projection[layer], core * heads_local)
        w_in = gathered(jnp.concatenate([zx[:, 0], zx[:, 1], maps, steps], axis=1))
        broad = low_broad[layer].reshape(own_rows, 3, half)
        shared = low_shared[layer].reshape(own_rows, -1)
        adapt = gathered(
            jnp.concatenate(
                [
                    broad[:, 0],
                    broad[:, 1],
                    lax.dynamic_slice_in_dim(shared, width + core * states, states, 1),
                    lanes_of(low_step[layer].reshape(own_rows, heads_local), core * heads_local),
                    broad[:, 2],
                    lax.dynamic_slice_in_dim(shared, core * part, part, 1),
                    lax.dynamic_slice_in_dim(shared, width + 2 * states + core * part, part, 1),
                ],
                axis=1,
            )
        )
        w_out = gathered(output_projection[layer].T)
        weights.append((w_in, adapt, w_out))

    def over_cores(values):
        return lax.all_gather(values, "mp", axis=values.ndim - 1, tiled=True)

    taps_all = jnp.concatenate([over_cores(head_conv_taps), map_conv_taps], axis=2).astype(full)
    gains_two = over_cores(gated_norm_gain).astype(full)
    tables = over_cores(head_settings)
    head_of = jnp.arange(inner)[None, :] // head_width
    spread_one = (jnp.arange(LANES)[:, None] == head_of).astype(low)
    spread_two = jnp.concatenate([spread_one, spread_one], axis=0)

    begin = place * length
    ends = jnp.concatenate([jnp.full((PAD,), -1, jnp.int32), documents, jnp.full((PAD,), -2, jnp.int32)])
    near = lax.dynamic_slice_in_dim(ends, begin, length + 2 * PAD)
    own = near[PAD : PAD + length]
    jump = jnp.where(own != near[PAD - 1 : PAD - 1 + length], RESET, 0.0).astype(full)
    jump = jnp.broadcast_to(jump[:, None], (length, LANES))

    def same_as(lag):
        same = (own == near[PAD + lag : PAD + lag + length]).astype(full)
        return jnp.broadcast_to(same[:, None], (length, LANES))

    lags = jnp.concatenate([same_as(-lag) for lag in range(1, CONV)], axis=1)
    leads = jnp.concatenate([same_as(lag) for lag in range(1, CONV)], axis=1)
    which = jnp.arange(ranks)[None, :] // rank
    mask = jnp.zeros((length, ranks), jnp.bool_)
    for document in range(chosen.shape[0]):
        mask = mask | ((own == document)[:, None] & (which == chosen[document]))
    mask = mask.astype(low)

    places = jnp.arange(pieces)
    distances = rows_of(jnp.arange(1, pieces), max(PAD, pieces))[:, None]
    earlier = ((places[None] < place) & (places[None] > place - distances)).astype(full)
    later = ((places[None] > place) & (places[None] < place + distances)).astype(full)

    def weigh(chooser, totals):
        return jnp.sum(chooser[:, :, None] * totals[None], axis=1)

    flops_in = 2 * length * width * (2 * inner + 3 * LANES)
    flops_out = 2 * length * width * inner
    flops_scan = 4 * length * SPAN * inner

    h = h_first
    kept = []
    for layer in range(layers):
        w_in, adapt, w_out = weights[layer]
        gain = rows_of(input_norm_gain[layer].astype(full)[None])
        taps = rows_of(taps_all[layer])
        gain_two = rows_of(gains_two[layer][None])
        table = rows_of(jnp.pad(tables[layer], ((0, 0), (0, LANES - heads))))
        skip = rows_of(jnp.repeat(tables[layer][2], head_width)[None])
        normed, spread, gate, rows, dt_raw = kernel_call(
            functools.partial(project_kernel, halves, half),
            [
                shape((length, width), low),
                shape((length, ranks), low),
                shape((length, inner), full),
                shape((length, channels), low),
                shape((length, LANES), full),
            ],
            [h, gain, mask, w_in, adapt],
            flops=flops_in,
            name="project",
        )
        halo = moved(rows[length - PAD :], "seq", 1)
        act, xdt, dt, cum, flat, begin_state, end_state, total = kernel_call(
            functools.partial(states_kernel, inner),
            [
                shape((length, channels), low),
                shape((length, inner), low),
                shape((length, LANES), full),
                shape((length, LANES), full),
                shape((LANES, length), full),
                shape((length // SPAN, states, inner), low),
                shape((states, inner), low),
                shape((PAD, LANES), full),
            ],
            [rows, halo, taps, lags, dt_raw, table, jump, spread_two],
            scratch=[pltpu.VMEM((length + PAD, channels), full), pltpu.VMEM((states, inner), full)],
            flops=flops_scan,
            name="states",
        )
        totals = lax.all_gather(total[0:1], "seq", axis=0, tiled=True)
        arrived = [moved(end_state, "seq", d) for d in range(1, pieces)]
        y_local = kernel_call(
            functools.partial(intra_kernel, inner, head_width),
            [shape((length, inner), low)],
            [act, xdt, cum, flat, begin_state, skip, spread_two],
            flops=flops_scan,
            name="intra",
        )[0]
        last = layer == layers - 1
        h_next, y, normal, spread_out, coming = kernel_call(
            functools.partial(output_kernel, halves, half, len(arrived), last),
            [
                shape((length, width), low if last else full),
                shape((length, inner), low),
                shape((length, inner), low),
                shape((length, ranks), low),
                shape((states, inner), low),
            ],
            [h, y_local, gate, act, cum, weigh(earlier, totals), gain_two, mask, w_out, adapt, spread_two, *arrived],
            scratch=[pltpu.VMEM((8, LANES), full)],
            flops=flops_out,
            name="output",
        )
        kept.append(
            (h, gain, taps, gain_two, table, skip, normed, spread, gate, rows, halo, dt_raw, act, xdt, dt, cum, flat,
             begin_state, totals, y, normal, spread_out, coming)
        )
        h = h_next
    mixed_own = h

    upstream = cotangent
    shares = [None] * layers
    for layer in reversed(range(layers)):
        w_in, adapt, w_out = weights[layer]
        (h, gain, taps, gain_two, table, skip, normed, spread, gate, rows, halo, dt_raw, act, xdt, dt, cum, flat,
         begin_state, totals, y, normal, spread_out, coming) = kept[layer]
        dgate, dy, own_grad, g_down_out, g_up_out = kernel_call(
            functools.partial(output_back_kernel, halves, half),
            [
                shape((length, inner), low),
                shape((length, inner), low),
                shape((states, inner), low),
                shape((halves, ranks, half), low),
                shape((halves, ranks, part), low),
            ],
            [upstream, y, gate, normal, spread_out, act, cum, gain_two, mask, w_out, adapt, spread_two],
            scratch=[pltpu.VMEM((length, ranks), low)],
            flops=flops_out,
            name="output_back",
        )
        arrived = [moved(own_grad, "seq", -d) for d in range(1, pieces)]
        early = jnp.concatenate([g_down_out, g_up_out], axis=2)
        u, db, dc = kernel_call(
            functools.partial(intra_back_kernel, inner, head_width),
            [shape((length, inner), low), shape((length, LANES), full), shape((length, LANES), full)],
            [act, xdt, dy, cum, flat],
            flops=2 * flops_scan,
            name="intra_back",
        )
        dn, dl, g_gate = kernel_call(
            functools.partial(gate_back_kernel, halves, half),
            [shape((length, width), full), shape((length, ranks), full), shape((halves, ranks, half), low)],
            [dgate, spread, w_in, adapt],
            flops=flops_in // 2,
            name="gate_back",
        )
        dconv, ddt = kernel_call(
            functools.partial(scan_back_kernel, inner, len(arrived)),
            [shape((length, channels), low), shape((length, LANES), low)],
            [rows, halo, taps, lags, act, xdt, dy, y, u, db, dc, dt, cum, dt_raw, table, skip, begin_state, coming,
             weigh(later, totals), spread_two, *arrived],
            scratch=[
                pltpu.VMEM((length + PAD, channels), full),
                pltpu.VMEM((states, inner), full),
                pltpu.VMEM((length, channels), full),
            ],
            flops=2 * flops_scan,
            name="scan_back",
        )
        after = moved(dconv[:PAD], "seq", -1)
        dh, g_rest, g_down_in = kernel_call(
            functools.partial(project_back_kernel, halves, half),
            [
                shape((length, width), full if layer > 0 else low),
                shape((halves, ranks, half + 2 * LANES), low),
                shape((halves, ranks, part), low),
            ],
            [upstream, h, gain, mask, dconv, after, taps, leads, ddt, dn, dl, spread, normed, w_in, adapt],
            scratch=[pltpu.VMEM((length + PAD, channels), full), pltpu.VMEM((length, channels), low)],
            flops=flops_in // 2,
            name="project_back",
        )
        upstream = dh
        rest = jnp.concatenate([g_gate, g_rest, g_down_in], axis=2)
        shares[layer] = jnp.concatenate([reduced(rest), reduced(early)], axis=1)

    whole = lax.all_gather(jnp.stack(shares), "seq", axis=1, tiled=True)
    zx, maps, steps, down_in, down_out, up_out = jnp.split(
        whole,
        [2 * half, 2 * half + LANES, 2 * half + 2 * LANES, 2 * half + 2 * LANES + part, 3 * half + 2 * LANES + part],
        axis=2,
    )
    own_shared = jnp.concatenate([maps, down_in, up_out], axis=2)
    other_shared = swapped(own_shared)
    in_order = [jnp.where(core == m, own_shared, other_shared) for m in range(halves)]
    maps, down_in, up_out = (
        [entry[:, :, first:last] for entry in in_order]
        for first, last in ((0, LANES), (LANES, LANES + part), (LANES + part, LANES + 2 * part))
    )
    shared_gradient = jnp.concatenate([*down_in, *maps, *up_out], axis=2).reshape(adapter_shared.shape)
    broad_gradient = jnp.concatenate([zx, down_out], axis=2).reshape(adapter_broad.shape)
    step_gradient = lax.dynamic_slice_in_dim(steps, core * heads_local, heads_local, 2).reshape(adapter_step.shape)
    local_sq = (
        jnp.sum(broad_gradient * broad_gradient)
        + jnp.sum(step_gradient * step_gradient)
        + jnp.sum(own_shared * own_shared)
    )
    squares = jnp.broadcast_to(local_sq, (8, LANES))
    squares = squares + swapped(squares)
    total_sq = squares
    for distance in range(1, owners):
        total_sq = total_sq + moved(squares, "dp", distance, True)
    grad_norm = jnp.sqrt(total_sq[0, 0])
    scale_factor = clip_max / jnp.maximum(grad_norm, clip_max)
    revised_broad, fresh_first_broad, fresh_square_broad = adamw_update(
        adapter_broad, broad_gradient, broad_first_moment, broad_second_moment, scale_factor
    )
    revised_step, fresh_first_step, fresh_square_step = adamw_update(
        adapter_step, step_gradient, step_first_moment, step_second_moment, scale_factor
    )
    revised_shared, fresh_first_shared, fresh_square_shared = adamw_update(
        adapter_shared, shared_gradient, shared_first_moment, shared_second_moment, scale_factor
    )

    def both(values):
        other = swapped(values)
        return jnp.stack([jnp.where(core == m, values, other) for m in range(halves)])[:, None]

    return (
        both(mixed_own),
        both(upstream),
        grad_norm,
        revised_broad,
        revised_step,
        revised_shared,
        fresh_first_broad,
        fresh_first_step,
        fresh_first_shared,
        fresh_square_broad,
        fresh_square_step,
        fresh_square_shared,
        revised_broad.astype(low),
        revised_step.astype(low),
        revised_shared.astype(low),
    )


def solution(mesh):
    placed = (
        P(None, "dp", "seq", None),
        P(None, "dp", "seq", None),
        P(None, "dp", None),
        P(None, "dp", None),
        P(),
        P(None, "dp", None, "mp"),
        P(None, "dp", None),
        P(None, "dp", "mp"),
        P(None, "mp", "dp"),
        P(None, None, "mp"),
        P(),
        P(None, None, "mp"),
        P(None, "mp"),
        P(None, "dp", None, None, "mp"),
        P(None, "dp", None, "mp"),
        P(None, "dp", None, None),
        P(None, "dp", None, None, "mp"),
        P(None, "dp", None, "mp"),
        P(None, "dp", None, None),
        P(None, "dp", None, None, "mp"),
        P(None, "dp", None, "mp"),
        P(None, "dp", None, None),
    )
    return jax.shard_map(
        per_device,
        mesh=mesh,
        in_specs=placed,
        out_specs=(
            P(None, "dp", "seq", None),
            P(None, "dp", "seq", None),
            P(),
            P(None, "dp", None, None, "mp"),
            P(None, "dp", None, "mp"),
            P(None, "dp", None, None),
            P(None, "dp", None, None, "mp"),
            P(None, "dp", None, "mp"),
            P(None, "dp", None, None),
            P(None, "dp", None, None, "mp"),
            P(None, "dp", None, "mp"),
            P(None, "dp", None, None),
            P(None, "dp", None, None, "mp"),
            P(None, "dp", None, "mp"),
            P(None, "dp", None, None),
        ),
        check_vma=False,
    )
```

time: 1370 us -> 564 us (0.41)
  matrix products: 365 us -> 0 us
  blocking collectives: 285 us -> 45.7 us
  other arithmetic: 234 us -> 22.3 us
  Pallas kernels: 0 us -> 163 us
  local copies, waits for them, and re-layouts: 200 us -> 78.1 us
  waiting for transfers between devices: 212 us -> 140 us
  starting transfers between devices: 25.4 us -> 83.5 us
    dot_general x166 -> x0, matrix products: 365 us -> none  [the longest x12 106 us: piece_ssd(): jnp.einsum('btsh,bshp->bthp', mixing, x_blocks, precision=highest)]
    pallas_call x0 -> x18, Pallas kernels: none -> 163 us  [kernel_call(): pl.pallas_call(body, out_shape=tuple(outs), in_specs=[whole] * len(ins),...]
    all_gather x14 -> x6, blocking collectives: 208 us -> 45.7 us  [the longest x2 26.7 us: per_device(): totals = lax.all_gather(total[0:1], 'seq', axis=0, tiled=True)]
    unnamed x18 -> x6, waiting for transfers between devices: 140 us -> 0.6 us
    ppermute x8 -> x51, starting transfers between devices: 22.8 us -> 83.3 us  [the longest x43 82 us: moved(): return lax.ppermute(block, axis, route)]
    psum x8 -> x0, blocking collectives: 59.3 us -> none  [the longest x1 16.9 us: per_device(): grad_norm = jnp.sqrt(lax.psum(local_sq, ('dp', 'mp')))]
    all_gather x12 -> x6, waiting for transfers between devices: 45.5 us -> 104 us  [gathered(): got = lax.all_gather(block, ('mp', 'dp'), axis=0, tiled=True)]
    another operation x44 -> x5, other arithmetic: 53.3 us -> 1.38 us  [the longest x2 1.35 us: both(): jnp.stack([jnp.where(core == m, values, other) for m in range(halves)])]
  transfers between devices with their start and end apart: 25 -> 57, of which waited for: 12 -> 21; matrix products, arithmetic and copies ran while one was open for 30% -> 8% of each run, Pallas kernels for 0% -> 26%
where the time goes in v1:
time: 564 us; the launch traced here: 553 us
  Pallas kernels  163 us (29%)
  waiting for transfers between devices  140 us (25%)
  starting transfers between devices  83.5 us (15%)
  local copies, waits for them, and re-layouts  78.1 us (14%)
  blocking collectives  45.7 us (8%)
  other arithmetic  22.3 us (4%)
  between operations  20.4 us (4%)
    pallas_call x18, Pallas kernels, kernel_call(): pl.pallas_call(body, out_shape=tuple(outs), in_specs=[whole] * len(ins),...  163 us
    all_gather x6, waiting for transfers between devices, gathered(): got = lax.all_gather(block, ('mp', 'dp'), axis=0, tiled=True)  104 us
    ppermute x43, starting transfers between devices, moved(): return lax.ppermute(block, axis, route)  82 us
    unnamed x297, local copies, waits for them, and re-layouts  48.6 us
    ppermute x43, waiting for transfers between devices, moved(): return lax.ppermute(block, axis, route)  34.4 us
    all_gather x2, blocking collectives, per_device(): totals = lax.all_gather(total[0:1], 'seq', axis=0, tiled=True)  26.7 us
    all_gather x1, blocking collectives, per_device(): whole = lax.all_gather(jnp.stack(shares), 'seq', axis=1, tiled=True)  12.6 us
  transfers between devices with their start and end apart: 57, of which 21 were waited for; matrix products, arithmetic and copies ran while one was open for 8% of the time, Pallas kernels for 26%

profile of v1, /device:TPU:0, one launch (start us, length us, event | category | flops | bytes accessed | tf_op | source)
XLA Modules:
  0.0 553.4 jit_solution(2480294500898269705)
XLA Ops:
  42.3 60.0 %all-gather.9.cloned.1.call-done = bf16[1536,1792]{1,0:T(8,128)(2,1)} async-done(((bf16[192,1792]{1,0:T(8,128)(2,1)}), bf16[1536,1792]{1,0:T(8,128)(2,1)}) %all-gather.9.cloned.1.call-update) | async-done | bytes 5505040 | tf_op jit(solution)/shard_map/all_gather | solution.py:564
  103.7 7.7 %project.2 = (bf16[512,768]{1,0:T(8,128)(2,1)S(1)}, bf16[512,128]{1,0:T(8,128)(2,1)S(1)}, f32[512,1536]{1,0:T(8,128)}, bf16[512,1792]{1,0:T(8,128)(2,1)S(1)}, f32[512,128]{1,0:T(8,128)S(1)}) custom-call(bf16[512,768]{1,0:T(8,128)(2,1)S(1)} %dynamic-slice_bitcast_fusion.1.h, f32[8,768]{1,0:T(8,128)S(1)} %pad_convert_fusion.1.gain, ...), custom_call_target="tpu_custom_call" | custom-call | flops 2717908992 | bytes 14311424 | tf_op jit(solution)/shard_map/project/pallas_call | solution.py:83
  122.4 10.2 %states.2 = (bf16[512,1792]{1,0:T(8,128)(2,1)}, bf16[512,1536]{1,0:T(8,128)(2,1)S(1)}, f32[512,128]{1,0:T(8,128)S(1)}, f32[512,128]{1,0:T(8,128)S(1)}, f32[128,5...) custom-call(bf16[512,1792]{1,0:T(8,128)(2,1)} %copy-done.10, ...), custom_call_target="tpu_custom_call" | custom-call | flops 402653184 | bytes 10186752 | tf_op jit(solution)/shard_map/states/pallas_call | solution.py:83
  134.0 5.2 collective-permute-start.1
  148.7 10.7 %all-gather = f32[4,1,128]{2,1,0:T(1,128)S(1)} all-gather(f32[1,1,128]{2,1,0:T(1,128)S(1)} %slice_bitcast_fusion.15), channel_id=1, replica_groups=mesh['dp'=4,'seq'=4,'mp'=2] {'seq'}, dimensions={0}, use_global_device_ids=true | all-gather | bytes 2560 | tf_op jit(solution)/shard_map/all_gather | solution.py:676
  161.7 5.0 intra.2.y_local
  170.0 8.9 %output.2 = (f32[512,768]{1,0:T(8,128)S(1)}, bf16[512,1536]{1,0:T(8,128)(2,1)}, bf16[512,1536]{1,0:T(8,128)(2,1)}, bf16[512,128]{1,0:T(8,128)(2,1)S(1)}, bf16[128,1536]{1,0:T(8,128)(2,1)S(1)}) custom-call(bf16[512,768]{1,0:T(8,128)(2,1)S(1)} %copy-done.13, bf16[512,1536]{1,0:T(8,128)(2,1)} %copy-done.30, f32[512,1536]{1,0:T(8,128)} %get-tuple-element.90.gate, ...), custom_call_target="tpu_custom_call" | custom-call | flops 1207959552 | bytes 19058688 | tf_op jit(solution)/shard_map/output/pallas_call | solution.py:83
  180.4 40.2 %all-gather.15.cloned.1.call-done = bf16[1536,1792]{1,0:T(8,128)(2,1)} async-done(((bf16[192,1792]{1,0:T(8,128)(2,1)}), bf16[1536,1792]{1,0:T(8,128)(2,1)}) %all-gather.15.cloned.1.call-update) | async-done | bytes 5505040 | tf_op jit(solution)/shard_map/all_gather | solution.py:564
  222.7 9.2 %project.3 = (bf16[512,768]{1,0:T(8,128)(2,1)S(1)}, bf16[512,128]{1,0:T(8,128)(2,1)S(1)}, f32[512,1536]{1,0:T(8,128)}, bf16[512,1792]{1,0:T(8,128)(2,1)}, f32[512,128]{1,0:T(8,128)S(1)}) custom-call(f32[512,768]{1,0:T(8,128)S(1)} %get-tuple-element.93.h, f32[8,768]{1,0:T(8,128)S(1)} %copy-done.92, bf16[512,128]{1,0:T(8,128)(2,1)S(1)} %or_convert_fusion.mask, ...), custom_call_target="tpu_custom_call" | custom-call | flops 2717908992 | bytes 15097856 | tf_op jit(solution)/shard_map/project/pallas_call | solution.py:83
  244.0 10.3 %states.3 = (bf16[512,1792]{1,0:T(8,128)(2,1)}, bf16[512,1536]{1,0:T(8,128)(2,1)S(1)}, f32[512,128]{1,0:T(8,128)S(1)}, f32[512,128]{1,0:T(8,128)S(1)}, f32[128,5...) custom-call(bf16[512,1792]{1,0:T(8,128)(2,1)} %get-tuple-element.94.rows, ...), custom_call_target="tpu_custom_call" | custom-call | flops 402653184 | bytes 10186752 | tf_op jit(solution)/shard_map/states/pallas_call | solution.py:83
  255.7 5.0 collective-permute-start.5
  271.7 16.0 %all-gather.1 = f32[4,1,128]{2,1,0:T(1,128)S(1)} all-gather(f32[1,1,128]{2,1,0:T(1,128)S(1)} %slice_bitcast_fusion.14), channel_id=1, replica_groups=mesh['dp'=4,'seq'=4,'mp'=2] {'seq'}, dimensions={0}, use_global_device_ids=true | all-gather | bytes 2560 | tf_op jit(solution)/shard_map/all_gather | solution.py:676
  290.9 5.0 intra.3.y_local
  298.1 8.9 %output.3 = (bf16[512,768]{1,0:T(8,128)(2,1)S(1)}, bf16[512,1536]{1,0:T(8,128)(2,1)S(1)}, bf16[512,1536]{1,0:T(8,128)(2,1)}, bf16[512,128]{1,0:T(8,128)(2,1)S(1)}, bf16[128,1536]{1,0:T(8,128)(2,1)S(1)}) custom-call(f32[512,768]{1,0:T(8,128)} %copy-done.21, bf16[512,1536]{1,0:T(8,128)(2,1)} %copy-done.29, f32[512,1536]{1,0:T(8,128)} %get-tuple-element.101.gate, ...), custom_call_target="tpu_custom_call" | custom-call | flops 1207959552 | bytes 19058688 | tf_op jit(solution)/shard_map/output/pallas_call | solution.py:83
  308.9 11.4 %output_back.2 = (bf16[512,1536]{1,0:T(8,128)(2,1)S(1)}, bf16[512,1536]{1,0:T(8,128)(2,1)}, bf16[128,1536]{1,0:T(8,128)(2,1)S(1)}, bf16[2,128,768]{2,1,0:T(8,128)(2,1)S(1)}, bf16[2,128,384]{2,1,0:T(8,128)(2,1)S(1)}) custom-call(bf16[512,768]{1,0:T(8,128)(2,1)S(1)} %copy-done.15, bf16[512,1536]{1,0:T(8,128)(2,1)} %copy-done.26, ...), custom_call_target="tpu_custom_call" | custom-call | flops 1207959552 | bytes 18464768 | tf_op jit(solution)/shard_map/output_back/pallas_call | solution.py:83
  341.8 5.3 intra_back.2
  354.5 6.3 %collective-permute-done.9.rest_0_ = bf16[128,1536]{1,0:T(8,128)(2,1)S(1)} collective-permute-done((bf16[128,1536]{1,0:T(8,128)(2,1)S(1)}, bf16[128,1536]{1,0:T(8,128)(2,1)S(1)}, u32[]{:S(2)}, u32[]{:S(2)}) %collective-permute-start.9) | collective-permute-done | bytes 393248 | tf_op jit(solution)/shard_map/ppermute | solution.py:460
  360.9 17.5 %scan_back.2 = (bf16[512,1792]{1,0:T(8,128)(2,1)}, bf16[512,128]{1,0:T(8,128)(2,1)S(1)}) custom-call(bf16[512,1792]{1,0:T(8,128)(2,1)} %get-tuple-element.94.rows, bf16[8,1792]{1,0:T(8,128)(2,1)S(1)} %copy-done.89, f32[8,1792]{1,0:T(8,128)S(1)} %copy-done.54, f32[512,384]{1,0:T(8,128)S(1)} %pad_maximum_fusion.lags, bf16[512,1792]{1,0:T(8,128)(2,1)} %get-tuple-element.96.act, ...), custom_call_target="tpu_custom_call" | custom-call | flops 805306368 | bytes 18100224 | tf_op jit(solution)/shard_map/scan_back/pallas_call | solution.py:83
  385.5 10.9 %project_back.2 = (f32[512,768]{1,0:T(8,128)S(1)}, bf16[2,128,1024]{2,1,0:T(8,128)(2,1)S(1)}, bf16[2,128,384]{2,1,0:T(8,128)(2,1)S(1)}) custom-call(bf16[512,768]{1,0:T(8,128)(2,1)S(1)} %copy-done.16, f32[512,768]{1,0:T(8,128)} %copy-done.21, f32[8,768]{1,0:T(8,128)S(1)} %copy-done.93, bf16[512,128]{1,0:T(8,128)(2,1)S(1)} %copy-done.20, ...), custom_call_target="tpu_custom_call" | custom-call | flops 1358954496 | bytes 17608704 | tf_op jit(solution)/shard_map/project_back/pallas_call | solution.py:83
  397.7 10.5 %output_back.3 = (bf16[512,1536]{1,0:T(8,128)(2,1)S(1)}, bf16[512,1536]{1,0:T(8,128)(2,1)S(1)}, bf16[128,1536]{1,0:T(8,128)(2,1)S(1)}, bf16[2,128,768]{2,1,0:T(8,128)(2,1)S(1)}, bf16[2,128,384]{2,1,0:T(8,128)(2,1)S(1)}) custom-call(f32[512,768]{1,0:T(8,128)} %copy-done.27, bf16[512,1536]{1,0:T(8,128)(2,1)} %get-tuple-element.123.y, ...), custom_call_target="tpu_custom_call" | custom-call | flops 1207959552 | bytes 19251200 | tf_op jit(solution)/shard_map/output_back/pallas_call | solution.py:83
  440.3 7.7 %collective-permute-done.15.rest_2_ = bf16[128,1536]{1,0:T(8,128)(2,1)S(1)} collective-permute-done((bf16[128,1536]{1,0:T(8,128)(2,1)S(1)}, bf16[128,1536]{1,0:T(8,128)(2,1)S(1)}, u32[]{:S(2)}, u32[]{:S(2)}) %collective-permute-start.15) | collective-permute-done | bytes 393248 | tf_op jit(solution)/shard_map/ppermute | solution.py:460
  448.1 17.4 %scan_back.3 = (bf16[512,1792]{1,0:T(8,128)(2,1)}, bf16[512,128]{1,0:T(8,128)(2,1)S(1)}) custom-call(bf16[512,1792]{1,0:T(8,128)(2,1)} %copy-done.10, bf16[8,1792]{1,0:T(8,128)(2,1)S(1)} %copy-done.86, f32[8,1792]{1,0:T(8,128)S(1)} %copy-done.52, f32[512,384]{1,0:T(8,128)S(1)} %pad_maximum_fusion.lags, bf16[512,1792]{1,0:T(8,128)(2,1)} %get-tuple-element.85.act, ...), custom_call_target="tpu_custom_call" | custom-call | flops 805306368 | bytes 18100224 | tf_op jit(solution)/shard_map/scan_back/pallas_call | solution.py:83
  472.0 10.5 %project_back.3 = (bf16[512,768]{1,0:T(8,128)(2,1)S(1)}, bf16[2,128,1024]{2,1,0:T(8,128)(2,1)S(1)}, bf16[2,128,384]{2,1,0:T(8,128)(2,1)S(1)}) custom-call(f32[512,768]{1,0:T(8,128)S(1)} %copy-done.28, bf16[512,768]{1,0:T(8,128)(2,1)S(1)} %copy-done.14, f32[8,768]{1,0:T(8,128)S(1)} %copy-done.91, bf16[512,128]{1,0:T(8,128)(2,1)S(1)} %copy-done.20, ...), custom_call_target="tpu_custom_call" | custom-call | flops 1358954496 | bytes 16822272 | tf_op jit(solution)/shard_map/project_back/pallas_call | solution.py:83
  509.2 12.6 %all_gather.47 = f32[2,32,3328]{2,0,1:T(2,128)S(1)} all-gather(f32[2,8,3328]{2,0,1:T(2,128)S(1)} %copy.245), channel_id=1, replica_groups=mesh['dp'=4,'seq'=4,'mp'=2] {'seq'}, dimensions={1}, use_global_device_ids=true | all-gather | bytes 1064960 | tf_op jit(solution)/shard_map/all_gather | solution.py:773
  (565 shorter events, 220.3 us)
Async XLA Ops:
  7.2 35.1 %all-gather.11.cloned.1.call-start = ((), (), s32[]{:S(2)}) async-start(), calls=%async_computation.1 | async-start | bytes 1916928 | tf_op jit(solution)/shard_map/all_gather | solution.py:564
  13.6 88.7 %all-gather.9.cloned.1.call-start = ((), (), s32[]{:S(2)}) async-start(), calls=%async_computation | async-start | bytes 6193152 | tf_op jit(solution)/shard_map/all_gather | solution.py:564
  17.0 151.0 %all-gather.13.cloned.1.call-start = ((), (), s32[]{:S(2)}) async-start(), calls=%async_computation.2 | async-start | bytes 2654208 | tf_op jit(solution)/shard_map/all_gather | solution.py:564
  18.1 162.3 %all-gather.17.cloned.1.call-start = ((), (), s32[]{:S(2)}) async-start(), calls=%async_computation.4 | async-start | bytes 1916928 | tf_op jit(solution)/shard_map/all_gather | solution.py:564
  20.6 199.9 %all-gather.15.cloned.1.call-start = ((), (), s32[]{:S(2)}) async-start(), calls=%async_computation.3 | async-start | bytes 6193152 | tf_op jit(solution)/shard_map/all_gather | solution.py:564
  22.2 275.1 %all-gather.19.cloned.1.call-start = ((), (), s32[]{:S(2)}) async-start(), calls=%async_computation.5 | async-start | bytes 2654208 | tf_op jit(solution)/shard_map/all_gather | solution.py:564
  134.0 34.0 %collective-permute-start.1 = (bf16[128,1536]{1,0:T(8,128)(2,1)}, bf16[128,1536]{1,0:T(8,128)(2,1)}, u32[]{:S(2)}, u32[]{:S(2)}) collective-permute-start(bf16[128,1536]{1,0:T(8,128)(2,1)} %get-tuple-element.92), channel_id=1, source_target_pairs={{0,2},{2,4},{4,6},{1,3},{3,5},{5,7},{8,10},{10,12},{12,14},{9,11},... | collective-permute-start | bytes 1179656 | tf_op jit(solution)/shard_map/ppermute | solution.py:460
  139.2 28.8 %collective-permute-start.2 = (bf16[128,1536]{1,0:T(8,128)(2,1)}, bf16[128,1536]{1,0:T(8,128)(2,1)}, u32[]{:S(2)}, u32[]{:S(2)}) collective-permute-start(bf16[128,1536]{1,0:T(8,128)(2,1)} %get-tuple-element.92), channel_id=1, source_target_pairs={{0,4},{2,6},{1,5},{3,7},{8,12},{10,14},{9,13},{11,15},{16,20},{18,... | collective-permute-start | bytes 1179656 | tf_op jit(solution)/shard_map/ppermute | solution.py:460
  142.6 25.4 %collective-permute-start.3 = (bf16[128,1536]{1,0:T(8,128)(2,1)}, bf16[128,1536]{1,0:T(8,128)(2,1)}, u32[]{:S(2)}, u32[]{:S(2)}) collective-permute-start(bf16[128,1536]{1,0:T(8,128)(2,1)} %get-tuple-element.92), channel_id=1, source_target_pairs={{0,6},{1,7},{8,14},{9,15},{16,22},{17,23},{24,30},{25,31}} | collective-permute-start | bytes 1179656 | tf_op jit(solution)/shard_map/ppermute | solution.py:460
  255.7 41.6 %collective-permute-start.5 = (bf16[128,1536]{1,0:T(8,128)(2,1)}, bf16[128,1536]{1,0:T(8,128)(2,1)}, u32[]{:S(2)}, u32[]{:S(2)}) collective-permute-start(bf16[128,1536]{1,0:T(8,128)(2,1)} %get-tuple-element.103), channel_id=1, source_target_pairs={{0,2},{2,4},{4,6},{1,3},{3,5},{5,7},{8,10},{10,12},{12,14},{9,11},... | collective-permute-start | bytes 1179656 | tf_op jit(solution)/shard_map/ppermute | solution.py:460
  260.7 36.6 %collective-permute-start.6 = (bf16[128,1536]{1,0:T(8,128)(2,1)}, bf16[128,1536]{1,0:T(8,128)(2,1)}, u32[]{:S(2)}, u32[]{:S(2)}) collective-permute-start(bf16[128,1536]{1,0:T(8,128)(2,1)} %get-tuple-element.103), channel_id=1, source_target_pairs={{0,4},{2,6},{1,5},{3,7},{8,12},{10,14},{9,13},{11,15},{16,20},{18,... | collective-permute-start | bytes 1179656 | tf_op jit(solution)/shard_map/ppermute | solution.py:460
  264.1 33.2 %collective-permute-start.7 = (bf16[128,1536]{1,0:T(8,128)(2,1)}, bf16[128,1536]{1,0:T(8,128)(2,1)}, u32[]{:S(2)}, u32[]{:S(2)}) collective-permute-start(bf16[128,1536]{1,0:T(8,128)(2,1)} %get-tuple-element.103), channel_id=1, source_target_pairs={{0,6},{1,7},{8,14},{9,15},{16,22},{17,23},{24,30},{25,31}} | collective-permute-start | bytes 1179656 | tf_op jit(solution)/shard_map/ppermute | solution.py:460
  325.8 25.8 %collective-permute-start.11 = (bf16[128,1536]{1,0:T(8,128)(2,1)}, bf16[128,1536]{1,0:T(8,128)(2,1)S(1)}, u32[]{:S(2)}, u32[]{:S(2)}) collective-permute-start(bf16[128,1536]{1,0:T(8,128)(2,1)} %copy-done.94), channel_id=1, source_target_pairs={{6,0},{7,1},{14,8},{15,9},{22,16},{23,17},{30,24},{31,25}} | collective-permute-start | bytes 1179656 | tf_op jit(solution)/shard_map/ppermute | solution.py:460
  349.7 80.5 %collective-permute-start.8 = (bf16[512,768]{1,0:T(8,128)(2,1)S(1)}, bf16[512,768]{1,0:T(8,128)(2,1)}, u32[]{:S(2)}, u32[]{:S(2)}) collective-permute-start(bf16[512,768]{1,0:T(8,128)(2,1)S(1)} %copy-done.60), channel_id=1, source_target_pairs={{0,1},{1,0},{2,3},{3,2},{4,5},{5,4},{6,7},{7,6},{8,9},{9,8},{10,11... | collective-permute-start | bytes 2359304 | tf_op jit(solution)/shard_map/ppermute | solution.py:465
  349.8 30.8 %collective-permute-start.43 = (bf16[8,1152]{1,0:T(8,128)(2,1)S(1)}, bf16[8,1152]{1,0:T(8,128)(2,1)S(1)}, u32[]{:S(2)}, u32[]{:S(2)}) collective-permute-start(bf16[8,1152]{1,0:T(8,128)(2,1)S(1)} %get-tuple-element.307), channel_id=1, source_target_pairs={{0,8},{8,16},{16,24},{24,0},{1,9},{9,17},{17,25},{25,1},{2,10},{10... | collective-permute-start | bytes 55304 | tf_op jit(solution)/shard_map/ppermute | solution.py:460
  349.9 30.7 %collective-permute-start.44 = (bf16[8,1152]{1,0:T(8,128)(2,1)S(1)}, bf16[8,1152]{1,0:T(8,128)(2,1)S(1)}, u32[]{:S(2)}, u32[]{:S(2)}) collective-permute-start(bf16[8,1152]{1,0:T(8,128)(2,1)S(1)} %get-tuple-element.309), channel_id=1, source_target_pairs={{0,16},{8,24},{16,0},{24,8},{1,17},{9,25},{17,1},{25,9},{2,18},{10... | collective-permute-start | bytes 55304 | tf_op jit(solution)/shard_map/ppermute | solution.py:460
  351.6 29.0 %collective-permute-start.45 = (bf16[8,1152]{1,0:T(8,128)(2,1)S(1)}, bf16[8,1152]{1,0:T(8,128)(2,1)S(1)}, u32[]{:S(2)}, u32[]{:S(2)}) collective-permute-start(bf16[8,1152]{1,0:T(8,128)(2,1)S(1)} %get-tuple-element.308), channel_id=1, source_target_pairs={{0,24},{8,0},{16,8},{24,16},{1,25},{9,1},{17,9},{25,17},{2,26},{10... | collective-permute-start | bytes 55304 | tf_op jit(solution)/shard_map/ppermute | solution.py:460
  408.2 27.9 %collective-permute-start.13 = (bf16[128,1536]{1,0:T(8,128)(2,1)S(1)}, bf16[128,1536]{1,0:T(8,128)(2,1)S(1)}, u32[]{:S(2)}, u32[]{:S(2)}) collective-permute-start(bf16[128,1536]{1,0:T(8,128)(2,1)S(1)} %get-tuple-element.132), channel_id=1, source_target_pairs={{2,0},{4,2},{6,4},{3,1},{5,3},{7,5},{10,8},{12,10},{14,12},{11,9},... | collective-permute-start | bytes 1179656 | tf_op jit(solution)/shard_map/ppermute | solution.py:460
  409.5 28.3 %collective-permute-start.14 = (bf16[128,1536]{1,0:T(8,128)(2,1)S(1)}, bf16[128,1536]{1,0:T(8,128)(2,1)S(1)}, u32[]{:S(2)}, u32[]{:S(2)}) collective-permute-start(bf16[128,1536]{1,0:T(8,128)(2,1)S(1)} %get-tuple-element.132), channel_id=1, source_target_pairs={{4,0},{6,2},{5,1},{7,3},{12,8},{14,10},{13,9},{15,11},{20,16},{22,... | collective-permute-start | bytes 1179656 | tf_op jit(solution)/shard_map/ppermute | solution.py:460
  435.8 46.8 %collective-permute-start.32 = (bf16[128,2176]{1,0:T(8,128)(2,1)S(1)}, bf16[128,2176]{1,0:T(8,128)(2,1)S(1)}, u32[]{:S(2)}, u32[]{:S(2)}) collective-permute-start(bf16[128,2176]{1,0:T(8,128)(2,1)S(1)} %copy-done.104), channel_id=1, source_target_pairs={{0,1},{1,0},{2,3},{3,2},{4,5},{5,4},{6,7},{7,6},{8,9},{9,8},{10,11... | collective-permute-start | bytes 1671176 | tf_op jit(solution)/shard_map/ppermute | solution.py:465
  436.0 31.8 %collective-permute-start.29 = (bf16[8,1152]{1,0:T(8,128)(2,1)S(1)}, bf16[8,1152]{1,0:T(8,128)(2,1)S(1)}, u32[]{:S(2)}, u32[]{:S(2)}) collective-permute-start(bf16[8,1152]{1,0:T(8,128)(2,1)S(1)} %get-tuple-element.304), channel_id=1, source_target_pairs={{0,8},{8,16},{16,24},{24,0},{1,9},{9,17},{17,25},{25,1},{2,10},{10... | collective-permute-start | bytes 55304 | tf_op jit(solution)/shard_map/ppermute | solution.py:460
  436.1 31.7 %collective-permute-start.30 = (bf16[8,1152]{1,0:T(8,128)(2,1)S(1)}, bf16[8,1152]{1,0:T(8,128)(2,1)S(1)}, u32[]{:S(2)}, u32[]{:S(2)}) collective-permute-start(bf16[8,1152]{1,0:T(8,128)(2,1)S(1)} %get-tuple-element.306), channel_id=1, source_target_pairs={{0,16},{8,24},{16,0},{24,8},{1,17},{9,25},{17,1},{25,9},{2,18},{10... | collective-permute-start | bytes 55304 | tf_op jit(solution)/shard_map/ppermute | solution.py:460
  437.8 30.0 %collective-permute-start.31 = (bf16[8,1152]{1,0:T(8,128)(2,1)S(1)}, bf16[8,1152]{1,0:T(8,128)(2,1)S(1)}, u32[]{:S(2)}, u32[]{:S(2)}) collective-permute-start(bf16[8,1152]{1,0:T(8,128)(2,1)S(1)} %get-tuple-element.305), channel_id=1, source_target_pairs={{0,24},{8,0},{16,8},{24,16},{1,25},{9,1},{17,9},{25,17},{2,26},{10... | collective-permute-start | bytes 55304 | tf_op jit(solution)/shard_map/ppermute | solution.py:460
  485.9 39.1 %collective-permute-start.17 = (bf16[512,768]{1,0:T(8,128)(2,1)S(1)}, bf16[512,768]{1,0:T(8,128)(2,1)S(1)}, u32[]{:S(2)}, u32[]{:S(2)}) collective-permute-start(bf16[512,768]{1,0:T(8,128)(2,1)S(1)} %get-tuple-element.140), channel_id=1, source_target_pairs={{0,1},{1,0},{2,3},{3,2},{4,5},{5,4},{6,7},{7,6},{8,9},{9,8},{10,11... | collective-permute-start | bytes 2359304 | tf_op jit(solution)/shard_map/ppermute | solution.py:465
  (164 other events, 1766.8 us)
Sparse Core Ops, SparseCore 0:
  13.7 28.5 all-gather.10
  44.5 57.7 all-gather.8
  104.5 30.3 all-gather.12
  136.3 24.9 all-gather.16
  162.7 57.7 all-gather.14
  222.6 30.3 all-gather.18
